TPU v7x, 512 devices: a whole 4x4x16 slice. The times are simulated.
512 devices in a mesh: frame: 32 (over x_lo, z), head: 16 (over y, x_hi, core).
Axes of the slice: x: 4 (x_hi: 2, x_lo: 2; x = x_hi * 2 + x_lo), y: 4, z: 16, core: 2. Of those that a mesh axis runs over, the one named last changes fastest.
Arguments:
- query_rows: bfloat16 [12288, 6144], P('frame', 'head'), may hold values from -15 to 15
- key_rows: bfloat16 [12288, 6144], P('frame', 'head'), may hold values from -15 to 15
- value_rows: bfloat16 [12288, 6144], P('frame', 'head'), may hold values from -6 to 6
- windows: int32 [24, 3], replicated, may hold values from 0 to 1
- out_weight: bfloat16 [3072, 3072], P('head'), may hold values from -0.109375 to 0.109375
Outputs:
- mixed: bfloat16 [2, 12288, 3072], P(None, ('frame', 'head'))
All inputs are finite; a program needn't handle non-finite values.
Results may differ from a plain program's by a relative error of at most 0.0062.
Values may be sent and summed in bfloat16 or wider, within the bound.
A program may use at most 64 MiB of HBM per device.

v0:
```python
import math

import jax
import jax.numpy as jnp
from jax import lax
from jax.sharding import PartitionSpec as P

HD = 128
SEEDS = 2
TILE_F = 6
TILE_H = 8
TILE_W = 4
FRAME_TILES = 4


NEGATIVE = -1e30


def from_behind(block, axis, distance):
    devices = range(lax.axis_size(axis))
    route = [(i - distance, i) for i in devices if i - distance in devices]
    return lax.ppermute(block, axis, route)


def swapped(value, axis, stride):
    mask = 2**stride
    pairs = [(source, source ^ mask) for source in range(lax.axis_size(axis))]
    return lax.ppermute(value, axis, pairs)


def attend_head(query_head, nearby_keys, nearby_values, allowed, tile_size, scaling):
    row_count = query_head.shape[0]
    tile_count = row_count // tile_size
    scores = (
        jnp.einsum("qd,kd->qk", query_head, nearby_keys, preferred_element_type=jnp.float32)
        * scaling
    )
    scores = scores.reshape(tile_count, tile_size, 9, tile_count, tile_size)
    scores = jnp.where(allowed[:, None, :, :, None], scores, NEGATIVE)
    scores = scores.reshape(row_count, 9 * row_count)
    row_peak = jnp.max(scores, axis=1, keepdims=True)
    weights = jnp.exp(scores - row_peak)
    denominator = jnp.sum(weights, axis=1, keepdims=True)
    rounded = weights.astype(jnp.bfloat16)
    return jnp.dot(rounded, nearby_values, preferred_element_type=jnp.float32) / denominator


def local(query_rows, key_rows, value_rows, windows, out_weight):
    row_count, local_width = query_rows.shape
    column_count = out_weight.shape[1]
    tile_size = TILE_F * TILE_H * TILE_W
    tile_count = row_count // tile_size
    heads_dev = local_width // HD
    head_total = lax.axis_size("head")
    groups = head_total // SEEDS
    head_pos = lax.axis_index("head")
    frame_pos = lax.axis_index("frame")
    frames = lax.axis_size("frame")
    row_tiles = frames // FRAME_TILES
    scaling = 1.0 / math.sqrt(HD)
    key_value = jnp.stack([key_rows, value_rows])
    slabs = []
    for frame_step in (-1, 0, 1):
        for row_step in (-1, 0, 1):
            if frame_step == 0 and row_step == 0:
                slabs.append(key_value)
            else:
                slabs.append(from_behind(key_value, "frame", -(frame_step * row_tiles + row_step)))
    nearby = jnp.concatenate(slabs, axis=1)
    counter = jnp.arange(tile_count, dtype=jnp.int32)
    col_near = jnp.abs(counter[:, None] - counter[None, :])
    step_list = jnp.array([-1, -1, -1, 0, 0, 0, 1, 1, 1], dtype=jnp.int32)
    row_list = jnp.array([-1, 0, 1, -1, 0, 1, -1, 0, 1], dtype=jnp.int32)
    frame_tile = frame_pos // row_tiles
    tile_row = frame_pos % row_tiles
    present = (
        (frame_tile + step_list >= 0)
        & (frame_tile + step_list < FRAME_TILES)
        & (tile_row + row_list >= 0)
        & (tile_row + row_list < row_tiles)
    )
    group_index = head_pos // SEEDS
    head_parts = []
    for head_slot in range(heads_dev):
        head_id = group_index * heads_dev + head_slot
        radius = lax.dynamic_slice(windows, (head_id, jnp.int32(0)), (1, 3))[0]
        allowed = (
            (jnp.abs(step_list)[None, :, None] <= radius[0])
            & (jnp.abs(row_list)[None, :, None] <= radius[1])
            & (col_near[:, None, :] <= radius[2])
            & present[None, :, None]
        )
        first_col = head_slot * HD
        head_parts.append(
            attend_head(
                query_rows[:, first_col : first_col + HD],
                nearby[0][:, first_col : first_col + HD],
                nearby[1][:, first_col : first_col + HD],
                allowed,
                tile_size,
                scaling,
            )
        )
    attended = jnp.concatenate(head_parts, axis=1).astype(jnp.bfloat16)
    partner_rows = swapped(out_weight, "head", 0)
    is_lower = head_pos % 2 == 0
    upper_half = jnp.where(is_lower, out_weight, partner_rows)
    lower_half = jnp.where(is_lower, partner_rows, out_weight)
    group_rows = jnp.concatenate([upper_half, lower_half], axis=0)
    partial_value = jnp.dot(attended, group_rows, preferred_element_type=jnp.float32).astype(
        jnp.bfloat16
    )
    owned_rows = row_count // head_total
    received = lax.all_to_all(
        partial_value.reshape(head_total, owned_rows, column_count),
        "head",
        split_axis=0,
        concat_axis=0,
        tiled=True,
    )
    combined = (
        received.astype(jnp.float32).reshape(groups, SEEDS, owned_rows, column_count).sum(axis=0)
    )
    return combined.astype(jnp.bfloat16)


def solution(mesh):
    placed = (P("frame", "head"), P("frame", "head"), P("frame", "head"), P(), P("head", None))
    return jax.shard_map(
        local,
        mesh=mesh,
        in_specs=placed,
        out_specs=P(None, ("frame", "head"), None),
        check_vma=False,
    )
```

profile of v0, /device:TPU:7, one launch (start us, length us, event | category | flops | bytes accessed | tf_op | source)
XLA Modules:
  0.0 385.3 jit_solution(8230462111400408955)
XLA Ops:
  0.0 1.9 pad_maximum_fusion
  1.9 15.0 %collective-permute-start = (bf16[2,384,384]{2,1,0:T(8,128)(2,1)}, bf16[2,384,384]{2,1,0:T(8,128)(2,1)}, u32[]{:S(2)}, u32[]{:S(2)}) collective-permute-start(bf16[2,384,384]{2,1,0:T(8,128)(2,1)} %pad_maximum_fusion), channel_id=1, source_target_pairs={{0,144},{16,160},{32,176},{48,192},{64,208},{80,224},{96,240},{112... | collective-permute-start | bytes 1769480 | tf_op jit(solution)/shard_map/ppermute | solution.py:22
  16.9 1.9 collective-permute-start.1
  18.9 5.2 %collective-permute-start.2 = (bf16[2,384,384]{2,1,0:T(8,128)(2,1)}, bf16[2,384,384]{2,1,0:T(8,128)(2,1)}, u32[]{:S(2)}, u32[]{:S(2)}) collective-permute-start(bf16[2,384,384]{2,1,0:T(8,128)(2,1)} %pad_maximum_fusion), channel_id=1, source_target_pairs={{0,112},{16,128},{32,144},{48,160},{64,176},{80,192},{96,208},{112... | collective-permute-start | bytes 1769480 | tf_op jit(solution)/shard_map/ppermute | solution.py:22
  24.1 1.9 collective-permute-start.3
  26.0 5.5 %collective-permute-start.4 = (bf16[2,384,384]{2,1,0:T(8,128)(2,1)}, bf16[2,384,384]{2,1,0:T(8,128)(2,1)}, u32[]{:S(2)}, u32[]{:S(2)}) collective-permute-start(bf16[2,384,384]{2,1,0:T(8,128)(2,1)} %pad_maximum_fusion), channel_id=1, source_target_pairs={{16,0},{32,16},{48,32},{64,48},{80,64},{96,80},{112,96},{128,112},... | collective-permute-start | bytes 1769480 | tf_op jit(solution)/shard_map/ppermute | solution.py:22
  33.6 4.5 %compare_and_fusion.3 = (pred[9]{0:T(512)(128)(4,1)S(1)}, pred[9]{0:T(512)(128)(4,1)S(1)}, pred[9]{0:T(512)(128)(4,1)S(1)}) fusion(s32[9]{0:T(128)} %constant.80, s32[9]{0:T(128)} %constant.79, s32[]{:T(128)} %bitcast.1, s32[]{:T(128)} %bitcast, s32[]{:T(128)} %bitcast.13, s32[]{:T(128)} %bitcast.12, s32[]{:T(128)} %bitcast.9, s32[]{:T(128)} %bitcast.8), kind=kLoop, calls=%fused_computation.68 | loop fusion | flops 81 | bytes 123 | tf_op jit(solution)/shard_map/and | solution.py:88
  40.7 1.9 broadcast_in_dim.30
  42.6 6.8 %broadcast_in_dim.54 = pred[384,3456]{1,0:T(32,128)(4,1)} reshape(pred[2,192,9,2,192]{4,3,2,1,0:T(4,128)(4,1)S(1)} %broadcast_in_dim.30) | data formatting | bytes 2654208 | tf_op jit(solution)/shard_map/jit(_where)/broadcast_in_dim | solution.py:39
  49.4 3.8 copy.8
  53.2 1.9 broadcast_in_dim.56
  55.1 6.8 %broadcast_in_dim.57 = pred[384,3456]{1,0:T(32,128)(4,1)} reshape(pred[2,192,9,2,192]{4,3,2,1,0:T(4,128)(4,1)S(1)} %broadcast_in_dim.56) | data formatting | bytes 2654208 | tf_op jit(solution)/shard_map/jit(_where)/broadcast_in_dim | solution.py:39
  62.0 3.8 copy.9
  65.8 1.9 broadcast_in_dim.58
  67.7 6.8 %broadcast_in_dim.59 = pred[384,3456]{1,0:T(32,128)(4,1)} reshape(pred[2,192,9,2,192]{4,3,2,1,0:T(4,128)(4,1)S(1)} %broadcast_in_dim.58) | data formatting | bytes 2654208 | tf_op jit(solution)/shard_map/jit(_where)/broadcast_in_dim | solution.py:39
  74.5 2.8 copy.10
  77.4 167.8 %collective-permute-done = bf16[2,384,384]{2,1,0:T(8,128)(2,1)} collective-permute-done((bf16[2,384,384]{2,1,0:T(8,128)(2,1)}, bf16[2,384,384]{2,1,0:T(8,128)(2,1)}, u32[]{:S(2)}, u32[]{:S(2)}) %collective-permute-start) | collective-permute-done | bytes 589856 | tf_op jit(solution)/shard_map/ppermute | solution.py:22
  245.2 1.9 collective-permute-start.5
  248.3 2.1 collective-permute-start.6
  250.4 1.2 constant_dynamic-update-slice_fusion.7
  251.5 1.9 collective-permute-start.7
  253.5 1.2 constant_dynamic-update-slice_fusion.6
  254.7 2.9 collective-permute-start.8
  257.5 1.2 constant_dynamic-update-slice_fusion.5
  258.8 29.1 %collective-permute-done.4 = bf16[2,384,384]{2,1,0:T(8,128)(2,1)} collective-permute-done((bf16[2,384,384]{2,1,0:T(8,128)(2,1)}, bf16[2,384,384]{2,1,0:T(8,128)(2,1)}, u32[]{:S(2)}, u32[]{:S(2)}) %collective-permute-start.4) | collective-permute-done | bytes 589856 | tf_op jit(solution)/shard_map/ppermute | solution.py:22
  287.9 1.2 constant_dynamic-update-slice_fusion.3
  289.0 11.6 %collective-permute-done.5 = bf16[2,384,384]{2,1,0:T(8,128)(2,1)S(1)} collective-permute-done((bf16[2,384,384]{2,1,0:T(8,128)(2,1)}, bf16[2,384,384]{2,1,0:T(8,128)(2,1)S(1)}, u32[]{:S(2)}, u32[]{:S(2)}) %collective-permute-start.5) | collective-permute-done | bytes 589856 | tf_op jit(solution)/shard_map/ppermute | solution.py:22
  300.9 34.3 %collective-permute-done.7 = bf16[2,384,384]{2,1,0:T(8,128)(2,1)S(1)} collective-permute-done((bf16[2,384,384]{2,1,0:T(8,128)(2,1)}, bf16[2,384,384]{2,1,0:T(8,128)(2,1)S(1)}, u32[]{:S(2)}, u32[]{:S(2)}) %collective-permute-start.7) | collective-permute-done | bytes 589856 | tf_op jit(solution)/shard_map/ppermute | solution.py:22
  337.8 1.1 fusion.64
  339.0 1.1 fusion.63
  345.8 1.4 convolution_convert_fusion
  347.2 36.9 %all_to_all.5 = bf16[16,24,3072]{2,1,0:T(8,128)(2,1)S(1)} all-to-all(bf16[16,24,3072]{2,1,0:T(8,128)(2,1)S(1)} %bitcast.30), channel_id=1, replica_groups=mesh['frame'=32,'head'=16] {'head'}, dimensions={0} | all-to-all | bytes 4718592 | tf_op jit(solution)/shard_map/all_to_all | solution.py:114
  (40 shorter events, 15.5 us)
Async XLA Ops:
  1.9 243.3 %collective-permute-start = (bf16[2,384,384]{2,1,0:T(8,128)(2,1)}, bf16[2,384,384]{2,1,0:T(8,128)(2,1)}, u32[]{:S(2)}, u32[]{:S(2)}) collective-permute-start(bf16[2,384,384]{2,1,0:T(8,128)(2,1)} %pad_maximum_fusion), channel_id=1, source_target_pairs={{0,144},{16,160},{32,176},{48,192},{64,208},{80,224},{96,240},{112... | collective-permute-start | bytes 1769480 | tf_op jit(solution)/shard_map/ppermute | solution.py:22
  16.9 231.3 %collective-permute-start.1 = (bf16[2,384,384]{2,1,0:T(8,128)(2,1)}, bf16[2,384,384]{2,1,0:T(8,128)(2,1)}, u32[]{:S(2)}, u32[]{:S(2)}) collective-permute-start(bf16[2,384,384]{2,1,0:T(8,128)(2,1)} %pad_maximum_fusion), channel_id=1, source_target_pairs={{0,128},{16,144},{32,160},{48,176},{64,192},{80,208},{96,224},{112... | collective-permute-start | bytes 1769480 | tf_op jit(solution)/shard_map/ppermute | solution.py:22
  18.9 232.7 %collective-permute-start.2 = (bf16[2,384,384]{2,1,0:T(8,128)(2,1)}, bf16[2,384,384]{2,1,0:T(8,128)(2,1)}, u32[]{:S(2)}, u32[]{:S(2)}) collective-permute-start(bf16[2,384,384]{2,1,0:T(8,128)(2,1)} %pad_maximum_fusion), channel_id=1, source_target_pairs={{0,112},{16,128},{32,144},{48,160},{64,176},{80,192},{96,208},{112... | collective-permute-start | bytes 1769480 | tf_op jit(solution)/shard_map/ppermute | solution.py:22
  24.1 230.6 %collective-permute-start.3 = (bf16[2,384,384]{2,1,0:T(8,128)(2,1)}, bf16[2,384,384]{2,1,0:T(8,128)(2,1)}, u32[]{:S(2)}, u32[]{:S(2)}) collective-permute-start(bf16[2,384,384]{2,1,0:T(8,128)(2,1)} %pad_maximum_fusion), channel_id=1, source_target_pairs={{0,16},{16,32},{32,48},{48,64},{64,80},{80,96},{96,112},{112,128},... | collective-permute-start | bytes 1769480 | tf_op jit(solution)/shard_map/ppermute | solution.py:22
  26.0 261.9 %collective-permute-start.4 = (bf16[2,384,384]{2,1,0:T(8,128)(2,1)}, bf16[2,384,384]{2,1,0:T(8,128)(2,1)}, u32[]{:S(2)}, u32[]{:S(2)}) collective-permute-start(bf16[2,384,384]{2,1,0:T(8,128)(2,1)} %pad_maximum_fusion), channel_id=1, source_target_pairs={{16,0},{32,16},{48,32},{64,48},{80,64},{96,80},{112,96},{128,112},... | collective-permute-start | bytes 1769480 | tf_op jit(solution)/shard_map/ppermute | solution.py:22
  74.5 180.2 %copy-start.2 = (bf16[192,3072]{1,0:T(8,128)(2,1)S(1)}, bf16[192,3072]{1,0:T(8,128)(2,1)}, u32[]{:S(2)}) copy-start(bf16[192,3072]{1,0:T(8,128)(2,1)} %param.11) | copy-start | bytes 3538948
  74.5 184.2 %copy-start.3 = (bf16[384,384]{1,0:T(8,128)(2,1)S(1)}, bf16[384,384]{1,0:T(8,128)(2,1)}, u32[]{:S(2)}) copy-start(bf16[384,384]{1,0:T(8,128)(2,1)} %param.9) | copy-start | bytes 884740
  74.5 184.2 %copy-start.4 = (bf16[384,384]{1,0:T(8,128)(2,1)S(1)}, bf16[384,384]{1,0:T(8,128)(2,1)}, u32[]{:S(2)}) copy-start(bf16[384,384]{1,0:T(8,128)(2,1)} %param.8) | copy-start | bytes 884740
  245.2 55.5 %collective-permute-start.5 = (bf16[2,384,384]{2,1,0:T(8,128)(2,1)}, bf16[2,384,384]{2,1,0:T(8,128)(2,1)S(1)}, u32[]{:S(2)}, u32[]{:S(2)}) collective-permute-start(bf16[2,384,384]{2,1,0:T(8,128)(2,1)} %pad_maximum_fusion), channel_id=1, source_target_pairs={{112,0},{128,16},{144,32},{160,48},{176,64},{192,80},{208,96},{224... | collective-permute-start | bytes 1769480 | tf_op jit(solution)/shard_map/ppermute | solution.py:22
  248.3 52.5 %collective-permute-start.6 = (bf16[2,384,384]{2,1,0:T(8,128)(2,1)}, bf16[2,384,384]{2,1,0:T(8,128)(2,1)S(1)}, u32[]{:S(2)}, u32[]{:S(2)}) collective-permute-start(bf16[2,384,384]{2,1,0:T(8,128)(2,1)} %pad_maximum_fusion), channel_id=1, source_target_pairs={{128,0},{144,16},{160,32},{176,48},{192,64},{208,80},{224,96},{240... | collective-permute-start | bytes 1769480 | tf_op jit(solution)/shard_map/ppermute | solution.py:22
  251.5 83.7 %collective-permute-start.7 = (bf16[2,384,384]{2,1,0:T(8,128)(2,1)}, bf16[2,384,384]{2,1,0:T(8,128)(2,1)S(1)}, u32[]{:S(2)}, u32[]{:S(2)}) collective-permute-start(bf16[2,384,384]{2,1,0:T(8,128)(2,1)} %pad_maximum_fusion), channel_id=1, source_target_pairs={{144,0},{160,16},{176,32},{192,48},{208,64},{224,80},{240,96},{256... | collective-permute-start | bytes 1769480 | tf_op jit(solution)/shard_map/ppermute | solution.py:22
  254.7 90.8 %collective-permute-start.8 = (bf16[192,3072]{1,0:T(8,128)(2,1)S(1)}, bf16[192,3072]{1,0:T(8,128)(2,1)S(1)}, u32[]{:S(2)}, u32[]{:S(2)}) collective-permute-start(bf16[192,3072]{1,0:T(8,128)(2,1)S(1)} %copy-done.2), channel_id=1, source_target_pairs={{0,1},{1,0},{2,3},{3,2},{4,5},{5,4},{6,7},{7,6},{8,9},{9,8},{10,11... | collective-permute-start | bytes 3538952 | tf_op jit(solution)/shard_map/ppermute | solution.py:28
  335.3 1.3 copy-start
  335.3 1.4 copy-start.5
  335.9 1.9 copy-start.1
where the time goes:
time: 390 us; the launch traced here: 385 us
  waiting for transfers between devices  243 us (62%)
  local copies, waits for them, and re-layouts  46.1 us (12%)
  starting transfers between devices  38.3 us (10%)
  blocking collectives  36.9 us (9%)
  other arithmetic  13.1 us (3%)
  matrix products  7.63 us (2%)
    ppermute x8, waiting for transfers between devices, from_behind(): return lax.ppermute(block, axis, route)  243 us
    all_to_all x1, blocking collectives, local(): lax.all_to_all(partial_value.reshape(head_total, owned_rows, column_count...  36.9 us
    broadcast_in_dim x9, local copies, waits for them, and re-layouts, attend_head(): scores = jnp.where(allowed[:, None, :, :, None], scores, NEGATIVE)  36.6 us
    ppermute x8, starting transfers between devices, from_behind(): return lax.ppermute(block, axis, route)  35.4 us
  transfers between devices with their start and end apart: 9, of which 4 were waited for; matrix products, arithmetic and copies ran while one was open for 16% of the time, Pallas kernels for 0%

commit v1 on v0

v1 whole, which is shorter than its diff:
```python
import math

import jax
import jax.numpy as jnp
from jax import lax
from jax.experimental import pallas as pl
from jax.experimental.pallas import tpu as pltpu
from jax.sharding import PartitionSpec as P

HD = 128
SEEDS = 2
FRAME_TILES = 4
NEGATIVE = -1e30
MESH = pl.DeviceIdType.MESH
BF = jnp.bfloat16
F32 = jnp.float32

Z, Y = 16, 4
ROW_TILES = 8
HEADS_DEV = 3
TOK = 384
TILE = 192
D = 3072
W_ROWS = 192
OWN = 24
QUARTER = 96

CHAIN, OPPOSITE, FAR, FAR_SAME, FAR_LAST, ACROSS = 0, 1, 2, 3, 4, 5
KINDS = 8


def kernel(q_hbm, k_hbm, v_hbm, windows, w_hbm, out_ref, *scratch):
    (kv, q_s, w_all, att, att_all, acc_o, send_o, recv_o, m_s, l_s, acc_s) = scratch[:11]
    (local_sem, z_send, z_recv, y_send, y_recv, w_send, w_recv, f_send, f_recv) = scratch[11:]

    frame = lax.axis_index("frame")
    head = lax.axis_index("head")
    xl, z = frame // Z, frame % Z
    y, xh, c = head // 4, (head // 2) % 2, head % 2
    row = z % ROW_TILES
    upper = z // ROW_TILES
    step = 2 * c - 1
    forwards = upper == xl

    def at_z(distance):
        return (xl * Z + (z + distance + Z) % Z, head)

    def at_y(distance):
        return (frame, ((y + distance) % Y) * 4 + xh * 2 + c)

    across_x = ((1 - xl) * Z + z, head)
    other_core = (frame, y * 4 + xh * 2 + 1 - c)

    def at_final(k):
        return (frame, y * 4 + (xh + k // 2) % 2 * 2 + (c + k) % 2)

    def local_copies(h):
        cols = pl.ds(pl.multiple_of(h * HD, HD), HD)
        return [
            pltpu.make_async_copy(k_hbm.at[:, cols], kv.at[0, h, 0], local_sem.at[0, h]),
            pltpu.make_async_copy(v_hbm.at[:, cols], kv.at[0, h, 1], local_sem.at[1, h]),
            pltpu.make_async_copy(q_hbm.at[:, cols], q_s.at[h], local_sem.at[2, h]),
        ]

    my_rows = pl.ds(pl.multiple_of(c * W_ROWS, W_ROWS), W_ROWS)
    w_local = pltpu.make_async_copy(w_hbm, w_all.at[y, my_rows], local_sem.at[3, 0])
    for h in range(HEADS_DEV):
        for copy in local_copies(h):
            copy.start()
    w_local.start()

    barrier = pltpu.get_barrier_semaphore()
    partners = [at_z(1), at_z(-1), at_z(6), at_z(-6), across_x]
    partners += [at_y(1), at_y(2), at_y(3), at_final(1), at_final(2), at_final(3)]
    for partner in partners:
        pl.semaphore_signal(barrier, inc=1, device_id=partner, device_id_type=MESH)
    pl.semaphore_wait(barrier, len(partners))

    def remote(src, dst, send, recv, target):
        return pltpu.make_async_remote_copy(
            src_ref=src, dst_ref=dst, send_sem=send, recv_sem=recv, device_id=target, device_id_type=MESH
        )

    def z_copy(kind, h):
        source, slot, target = {
            CHAIN: (0, 2, at_z(step)),
            OPPOSITE: (0, 1, at_z(-step)),
            FAR: (2, 3, at_z(6 * step)),
            FAR_SAME: (3, 4, at_z(step)),
            FAR_LAST: (4, 5, at_z(step)),
            ACROSS: (3, 6, across_x),
            ACROSS + 1: (4, 7, across_x),
            ACROSS + 2: (5, 8, across_x),
        }[kind]
        return remote(kv.at[source, h], kv.at[slot, h], z_send.at[kind, h], z_recv.at[kind, h], target)

    def w_copy(k):
        return remote(w_hbm, w_all.at[y, my_rows], w_send.at[k], w_recv.at[k], at_y(k))

    def w_share(k):
        place = w_all.at[(y + Y - k) % Y, my_rows]
        return remote(place, place, w_send.at[Y + k], w_recv.at[Y + k], other_core)

    def y_copy(k, h):
        rows = pl.ds(pl.multiple_of((y + k) % Y * QUARTER, QUARTER), QUARTER)
        return remote(att.at[h, rows], att_all.at[y, h], y_send.at[k, h], y_recv.at[k, h], at_y(k))

    def f_copy(k, half):
        piece = (xh + k // 2) % 2 * 2 + (c + k) % 2
        return remote(
            send_o.at[half, piece], recv_o.at[half, k], f_send.at[half, k], f_recv.at[half, k], at_final(k)
        )

    for h in range(HEADS_DEV):
        for copy in local_copies(h):
            copy.wait()
        z_copy(CHAIN, h).start()
    for h in range(HEADS_DEV):
        z_copy(OPPOSITE, h).start()
    for k in range(1, Y):
        w_copy(k).start()
    w_local.wait()
    w_share(0).start()
    z_copy(CHAIN, 0).wait_recv()
    z_copy(FAR, 0).start()

    group = y * 2 + xh
    scaling = 1.0 / math.sqrt(HD)
    column = lax.broadcasted_iota(jnp.int32, (1, TOK), 1) // TILE

    def attend(h, slot, far_frame, far_row, first=False):
        head_id = group * HEADS_DEV + h
        allowed = (far_frame <= windows[head_id, 0]) & (far_row <= windows[head_id, 1])
        same = jnp.where(allowed, 0.0, NEGATIVE)
        other = jnp.where(allowed & (windows[head_id, 2] >= 1), 0.0, NEGATIVE)
        keys, values = kv[slot, h, 0], kv[slot, h, 1]
        for half in range(2):
            rows = pl.ds(half * TILE, TILE)
            bias = jnp.where(column == half, same, other)
            scores = lax.dot_general(
                q_s[h, rows], keys, (((1,), (1,)), ((), ())), preferred_element_type=F32
            )
            scores = scores * scaling + bias
            peak = jnp.max(scores, axis=1, keepdims=True)
            if not first:
                before = m_s[rows, :1]
                peak = jnp.maximum(peak, before)
            weights = jnp.exp(scores - peak)
            total = jnp.sum(weights, axis=1, keepdims=True)
            mixed = jnp.dot(weights.astype(BF), values, preferred_element_type=F32)
            if not first:
                fade = jnp.exp(before - peak)
                total += fade * l_s[rows, :1]
                mixed += fade * acc_s[rows]
            m_s[rows] = jnp.broadcast_to(peak, (TILE, HD))
            l_s[rows] = jnp.broadcast_to(total, (TILE, HD))
            acc_s[rows] = mixed

    def in_grid(r):
        return (r >= 0) & (r < ROW_TILES)

    ahead, behind = in_grid(row + step), in_grid(row - step)

    def one_head(h, carry):
        attend(h, 0, 0, 0, first=True)
        z_copy(OPPOSITE, h).wait_recv()

        @pl.when(behind)
        def _():
            attend(h, 2, 0, 1)

        @pl.when(ahead)
        def _():
            attend(h, 1, 0, 1)

        z_copy(FAR, h).wait_recv()
        z_copy(FAR_SAME, h).start()

        @pl.when(h < HEADS_DEV - 1)
        def _():
            z_copy(CHAIN, h + 1).wait_recv()
            z_copy(FAR, h + 1).start()

        @pl.when(forwards)
        def _():
            z_copy(ACROSS, h).start()

        @pl.when(ahead)
        def _():
            attend(h, 3, 1, 1)

        z_copy(FAR_SAME, h).wait_recv()
        z_copy(FAR_LAST, h).start()

        @pl.when(forwards)
        def _():
            z_copy(ACROSS + 1, h).start()

        attend(h, 4, 1, 0)
        z_copy(FAR_LAST, h).wait_recv()

        @pl.when(forwards)
        def _():
            z_copy(ACROSS + 2, h).start()

        @pl.when(behind)
        def _():
            attend(h, 5, 1, 1)

        @pl.when(h == HEADS_DEV - 1)
        def _():
            project_early()

        @pl.when(jnp.logical_not(forwards))
        def _():
            z_copy(ACROSS, h).wait_recv()

            @pl.when(ahead)
            def _():
                attend(h, 6, 1, 1)

            z_copy(ACROSS + 1, h).wait_recv()
            attend(h, 7, 1, 0)
            z_copy(ACROSS + 2, h).wait_recv()

            @pl.when(behind)
            def _():
                attend(h, 8, 1, 1)

        att[h] = (acc_s[...] / l_s[...]).astype(BF)
        for k in range(1, Y):
            y_copy(k, h).start()
        att_all[y, h] = att[h, pl.ds(pl.multiple_of(y * QUARTER, QUARTER), QUARTER)]
        return carry

    wide = D // 6

    def project_early():
        for k in range(1, Y):
            w_copy(k).wait_recv()
            w_share(k).start()
        for k in range(Y):
            w_share(k).wait_recv()
        for k in range(1, Y):
            for h in range(HEADS_DEV - 1):
                y_copy(k, h).wait_recv()
        depth = (HEADS_DEV - 1) * HD

        def part(i, carry):
            cols = pl.ds(pl.multiple_of(i * wide, wide), wide)
            total = jnp.zeros((QUARTER, wide), F32)
            for s in range(Y):
                rows = jnp.concatenate([att_all[s, h] for h in range(HEADS_DEV - 1)], axis=1)
                total += jnp.dot(rows, w_all[s, :depth, cols], preferred_element_type=F32)
            acc_o[:, cols] = total
            return carry

        lax.fori_loop(0, 6, part, 0)

    lax.fori_loop(0, HEADS_DEV, one_head, 0)

    last = HEADS_DEV - 1
    for k in range(1, Y):
        y_copy(k, last).wait_recv()
    half_wide, part_wide = D // 2, D // 4
    for half in range(2):
        for piece_col in range(2):
            cols = pl.ds(half * half_wide + piece_col * part_wide, part_wide)
            total = acc_o[:, cols]
            for s in range(Y):
                total += jnp.dot(
                    att_all[s, last], w_all[s, last * HD : (last + 1) * HD, cols], preferred_element_type=F32
                )
            for piece in range(4):
                send_o[half, piece, piece_col * OWN : (piece_col + 1) * OWN, :] = total[
                    piece * OWN : (piece + 1) * OWN
                ].astype(BF)
        for k in (2, 3, 1):
            f_copy(k, half).start()

    own = xh * 2 + c
    for half in range(2):
        for k in range(1, 4):
            f_copy(k, half).wait_recv()
        mine = send_o[half, own].astype(F32) + recv_o[half, 2].astype(F32)
        others = recv_o[half, 1].astype(F32) + recv_o[half, 3].astype(F32)
        mine, others = mine.astype(BF), others.astype(BF)
        for piece_col in range(2):
            cols = pl.ds(half * half_wide + piece_col * part_wide, part_wide)
            rows = slice(piece_col * OWN, (piece_col + 1) * OWN)
            out_ref[0, :, cols] = jnp.where(c == 0, mine[rows], others[rows])
            out_ref[1, :, cols] = jnp.where(c == 0, others[rows], mine[rows])

    def sent(h, carry):
        for kind in range(ACROSS):
            z_copy(kind, h).wait_send()

        @pl.when(forwards)
        def _():
            for kind in range(ACROSS, KINDS):
                z_copy(kind, h).wait_send()

        for k in range(1, Y):
            y_copy(k, h).wait_send()
        return carry

    lax.fori_loop(0, HEADS_DEV, sent, 0)
    for k in range(1, Y):
        w_copy(k).wait_send()
    for k in range(Y):
        w_share(k).wait_send()
    for half in range(2):
        for k in range(1, 4):
            f_copy(k, half).wait_send()


def local(query_rows, key_rows, value_rows, windows, out_weight):
    dma = pltpu.SemaphoreType.DMA
    anywhere = pl.BlockSpec(memory_space=pl.ANY)
    return pl.pallas_call(
        kernel,
        out_shape=jax.ShapeDtypeStruct((SEEDS, OWN, D), BF),
        in_specs=[anywhere] * 3 + [pl.BlockSpec(memory_space=pltpu.SMEM), anywhere],
        out_specs=pl.BlockSpec(memory_space=pltpu.VMEM),
        scratch_shapes=[
            pltpu.VMEM((9, HEADS_DEV, 2, TOK, HD), BF),
            pltpu.VMEM((HEADS_DEV, TOK, HD), BF),
            pltpu.VMEM((Y, 2 * W_ROWS, D), BF),
            pltpu.VMEM((HEADS_DEV, TOK, HD), BF),
            pltpu.VMEM((Y, HEADS_DEV, QUARTER, HD), BF),
            pltpu.VMEM((QUARTER, D), F32),
            pltpu.VMEM((2, 4, 2 * OWN, D // 4), BF),
            pltpu.VMEM((2, 4, 2 * OWN, D // 4), BF),
            pltpu.VMEM((TOK, HD), F32),
            pltpu.VMEM((TOK, HD), F32),
            pltpu.VMEM((TOK, HD), F32),
            dma((4, HEADS_DEV)),
            dma((KINDS, HEADS_DEV)),
            dma((KINDS, HEADS_DEV)),
            dma((Y, HEADS_DEV)),
            dma((Y, HEADS_DEV)),
            dma((2 * Y,)),
            dma((2 * Y,)),
            dma((2, 4)),
            dma((2, 4)),
        ],
        compiler_params=pltpu.CompilerParams(
            collective_id=0, has_side_effects=True, vmem_limit_bytes=48 << 20
        ),
        cost_estimate=pl.CostEstimate(
            flops=2 * (2 * HEADS_DEV * TOK * 9 * TOK * HD + TOK * HEADS_DEV * HD * D),
            bytes_accessed=4 << 20,
            transcendentals=HEADS_DEV * TOK * 9 * TOK,
        ),
    )(query_rows, key_rows, value_rows, windows, out_weight)


def solution(mesh):
    placed = (P("frame", "head"), P("frame", "head"), P("frame", "head"), P(), P("head", None))
    return jax.shard_map(
        local,
        mesh=mesh,
        in_specs=placed,
        out_specs=P(None, ("frame", "head"), None),
        check_vma=False,
    )
```

time: 390 us -> 137 us (0.35)
  waiting for transfers between devices: 243 us -> 0 us
  Pallas kernels: 0 us -> 128 us
  local copies, waits for them, and re-layouts: 46.1 us -> 5.63 us
  starting transfers between devices: 38.3 us -> 0 us
  blocking collectives: 36.9 us -> 0 us
  other arithmetic: 13.1 us -> 0 us
  matrix products: 7.63 us -> 0 us
    ppermute x9 -> x0, waiting for transfers between devices: 243 us -> none  [the longest x8 243 us: from_behind(): return lax.ppermute(block, axis, route)]
    pallas_call x0 -> x1, Pallas kernels: none -> 128 us  [local(): pl.pallas_call(kernel, out_shape=jax.ShapeDtypeStruct((SEEDS, OWN, D), BF...]
    ppermute x9 -> x0, starting transfers between devices: 38.3 us -> none  [the longest x8 35.4 us: from_behind(): return lax.ppermute(block, axis, route)]
    all_to_all x1 -> x0, blocking collectives: 36.9 us -> none  [local(): lax.all_to_all(partial_value.reshape(head_total, owned_rows, column_count...]
    broadcast_in_dim x9 -> x0, local copies, waits for them, and re-layouts: 36.6 us -> none  [attend_head(): scores = jnp.where(allowed[:, None, :, :, None], scores, NEGATIVE)]
    dot_general x7 -> x0, matrix products: 7.63 us -> none  [the longest x3 3.42 us: attend_head(): jnp.einsum('qd,kd->qk', query_head, nearby_keys, preferred_element_type=j...]
    and x3 -> x0, other arithmetic: 5.26 us -> none  [the longest x2 4.58 us: local(): (jnp.abs(step_list)[None, :, None] <= radius[0]) & (jnp.abs(row_list)[Non...]
  transfers between devices with their start and end apart: 9 -> 0, of which waited for: 4 -> 0; matrix products, arithmetic and copies ran while one was open for 16% -> 0% of each run, Pallas kernels for 0% -> 0%
where the time goes in v1:
time: 137 us; the launch traced here: 134 us
  Pallas kernels  128 us (93%)
  local copies, waits for them, and re-layouts  5.63 us (4%)
    pallas_call x1, Pallas kernels, local(): pl.pallas_call(kernel, out_shape=jax.ShapeDtypeStruct((SEEDS, OWN, D), BF...  128 us
    unnamed x10, local copies, waits for them, and re-layouts  5.63 us

profile of v1, /device:TPU:7, one launch (start us, length us, event | category | flops | bytes accessed | tf_op | source)
XLA Modules:
  0.0 134.1 jit_solution(16538053389939470516)
XLA Ops:
  0.0 0.8 copy.6.windows
  0.8 0.0 copy-start
  0.8 1.3 copy-done
  2.0 0.0 copy-start.1
  2.0 1.0 copy-done.1
  3.0 0.0 copy-start.2
  3.0 1.0 copy-done.2
  4.0 0.0 copy-start.3
  4.0 1.0 copy-done.3
  4.9 128.5 %shard_map.55 = bf16[2,24,3072]{2,1,0:T(8,128)(2,1)S(1)} custom-call(bf16[384,384]{1,0:T(8,128)(2,1)S(1)} %copy-done.1, bf16[384,384]{1,0:T(8,128)(2,1)S(1)} %copy-done.2, bf16[384,384]{1,0:T(8,128)(2,1)S(1)} %copy-done.3, s32[24,3]{1,0:T(8,128)S(1)} %copy.6.windows, bf16[192,3072]{1,0:T(8,128)(2,1)S(1)} %copy-done), custom_call_target="tpu_custom_call" | custom-call | flops 2944401408 | bytes 4194304 | tf_op jit(solution)/shard_map/pallas_call | solution.py:320
  133.4 0.7 copy.8
Async XLA Ops:
  0.8 1.3 copy-start
  2.0 1.0 copy-start.1
  3.0 1.0 copy-start.2
  4.0 1.0 copy-start.3

commit v2 on v1

v2 whole, which is shorter than its diff:
```python
import math

import jax
import jax.numpy as jnp
from jax import lax
from jax.experimental import pallas as pl
from jax.experimental.pallas import tpu as pltpu
from jax.sharding import PartitionSpec as P

HD = 128
SEEDS = 2
FRAME_TILES = 4
NEGATIVE = -1e30
MESH = pl.DeviceIdType.MESH
BF = jnp.bfloat16
F32 = jnp.float32

Z, Y = 16, 4
ROW_TILES = 8
HEADS_DEV = 3
TOK = 384
TILE = 192
D = 3072
W_ROWS = 192
OWN = 24
QUARTER = 96

CHAIN, OPPOSITE, LEAP, FAR, FAR_SAME, FAR_LAST = range(6)
ROUTES = ((0, 2, 1), (0, 1, -1), (2, 3, 3), (3, 4, 3), (4, 5, 1), (5, 6, 1))
SLOTS = 7
PARTS = 4
PART = D // PARTS
LOG2E = math.log2(math.e)


def kernel(q_hbm, k_hbm, v_hbm, windows, w_hbm, out_ref, *scratch):
    (kv, q_s, w_all, att, att_all, acc_o, send_o, recv_o, m_s, l_s, acc_s) = scratch[:11]
    (part_send, part_recv, lse_send, lse_recv) = scratch[11:15]
    (local_sem, z_send, z_recv, x_send, x_recv, y_send, y_recv, w_send, w_recv, f_send, f_recv) = scratch[15:]

    frame = lax.axis_index("frame")
    head = lax.axis_index("head")
    xl, z = frame // Z, frame % Z
    y, xh, c = head // 4, (head // 2) % 2, head % 2
    row = z % ROW_TILES
    upper = z // ROW_TILES
    step = 2 * c - 1
    helps = upper == xl
    helped = upper != xl

    def at_z(distance):
        return (xl * Z + (z + distance + Z) % Z, head)

    def at_y(distance):
        return (frame, ((y + distance) % Y) * 4 + xh * 2 + c)

    across_x = ((1 - xl) * Z + z, head)
    other_core = (frame, y * 4 + xh * 2 + 1 - c)

    def at_final(k):
        return (frame, y * 4 + (xh + k // 2) % 2 * 2 + (c + k) % 2)

    def local_copy(i, h):
        cols = pl.ds(pl.multiple_of(h * HD, HD), HD)
        source = (k_hbm, v_hbm, q_hbm)[i].at[:, cols]
        target = q_s.at[0, h] if i == 2 else kv.at[0, h, i]
        return pltpu.make_async_copy(source, target, local_sem.at[i, h])

    my_rows = pl.ds(pl.multiple_of(c * W_ROWS, W_ROWS), W_ROWS)
    w_local = pltpu.make_async_copy(w_hbm, w_all.at[y, my_rows], local_sem.at[3, 0])
    for i in range(3):
        for h in range(HEADS_DEV):
            local_copy(i, h).start()
    w_local.start()

    barrier = pltpu.get_barrier_semaphore()
    partners = [at_z(1), at_z(-1), at_z(3), at_z(-3), across_x]
    partners += [at_y(1), at_y(2), at_y(3), at_final(1), at_final(2), at_final(3)]
    for partner in partners:
        pl.semaphore_signal(barrier, inc=1, device_id=partner, device_id_type=MESH)
    pl.semaphore_wait(barrier, len(partners))

    def remote(src, dst, send, recv, target):
        return pltpu.make_async_remote_copy(
            src_ref=src, dst_ref=dst, send_sem=send, recv_sem=recv, device_id=target, device_id_type=MESH
        )

    def z_copy(kind, h):
        source, slot, hops = ROUTES[kind]
        return remote(
            kv.at[source, h], kv.at[slot, h], z_send.at[kind, h], z_recv.at[kind, h], at_z(hops * step)
        )

    def x_query(h):
        return remote(q_s.at[0, h], q_s.at[1, h], x_send.at[0, h], x_recv.at[0, h], across_x)

    def x_part(h):
        return remote(part_send.at[h], part_recv.at[h], x_send.at[1, h], x_recv.at[1, h], across_x)

    def x_lse(h):
        return remote(lse_send.at[h], lse_recv.at[h], x_send.at[2, h], x_recv.at[2, h], across_x)

    def w_copy(k):
        return remote(w_hbm, w_all.at[y, my_rows], w_send.at[k], w_recv.at[k], at_y(k))

    def w_share(k):
        place = w_all.at[(y + Y - k) % Y, my_rows]
        return remote(place, place, w_send.at[Y + k], w_recv.at[Y + k], other_core)

    def y_copy(k, h):
        rows = pl.ds(pl.multiple_of((y + k) % Y * QUARTER, QUARTER), QUARTER)
        return remote(att.at[h, rows], att_all.at[y, h], y_send.at[k, h], y_recv.at[k, h], at_y(k))

    def f_copy(k, part):
        piece = (xh + k // 2) % 2 * 2 + (c + k) % 2
        return remote(
            send_o.at[part, piece], recv_o.at[part, k], f_send.at[part, k], f_recv.at[part, k], at_final(k)
        )

    for h in range(HEADS_DEV):
        local_copy(0, h).wait()
        local_copy(1, h).wait()
        z_copy(CHAIN, h).start()
    for h in range(HEADS_DEV):
        z_copy(OPPOSITE, h).start()
    for h in range(HEADS_DEV):
        local_copy(2, h).wait()

        @pl.when(helped)
        def _():
            x_query(h).start()

    for k in range(1, Y):
        w_copy(k).start()
    w_local.wait()
    w_share(0).start()

    group = y * 2 + xh
    scaling = LOG2E / math.sqrt(HD)
    column = lax.broadcasted_iota(jnp.int32, (1, TOK), 1) // TILE

    def attend(owner, h, slot, far_frame, far_row, first=False):
        head_id = group * HEADS_DEV + h
        allowed = (far_frame <= windows[0, head_id]) & (far_row <= windows[1, head_id])
        same = jnp.where(allowed, 0.0, NEGATIVE)
        other = jnp.where(allowed & (windows[2, head_id] >= 1), 0.0, NEGATIVE)
        keys, values = kv[slot, h, 0], kv[slot, h, 1]
        for half in range(2):
            rows = pl.ds(half * TILE, TILE)
            bias = jnp.where(column == half, same, other)
            scores = lax.dot_general(
                q_s[owner, h, rows], keys, (((1,), (1,)), ((), ())), preferred_element_type=F32
            )
            scores = scores * scaling + bias
            peak = jnp.max(scores, axis=1, keepdims=True)
            if not first:
                before = m_s[owner, h, rows, :1]
                peak = jnp.maximum(peak, before)
            weights = jnp.exp2(scores - peak)
            total = jnp.sum(weights, axis=1, keepdims=True)
            mixed = jnp.dot(weights.astype(BF), values, preferred_element_type=F32)
            if not first:
                fade = jnp.exp2(before - peak)
                total += fade * l_s[owner, h, rows, :1]
                mixed += fade * acc_s[owner, h, rows]
            m_s[owner, h, rows] = jnp.broadcast_to(peak, (TILE, HD))
            l_s[owner, h, rows] = jnp.broadcast_to(total, (TILE, HD))
            acc_s[owner, h, rows] = mixed

    def in_grid(r):
        return (r >= 0) & (r < ROW_TILES)

    ahead, behind = in_grid(row + step), in_grid(row - step)

    def each_head(body):
        def run(h, carry):
            body(h)
            return carry

        lax.fori_loop(0, HEADS_DEV, run, 0)

    def hand_on(h):
        z_copy(CHAIN, h).wait_recv()
        z_copy(LEAP, h).start()

    def near(h):
        attend(0, h, 0, 0, 0, first=True)

        @pl.when(behind)
        def _():
            attend(0, h, 2, 0, 1)

    def near_opposite(h):
        z_copy(OPPOSITE, h).wait_recv()

        @pl.when(ahead)
        def _():
            attend(0, h, 1, 0, 1)

    def leap(h):
        z_copy(LEAP, h).wait_recv()
        z_copy(FAR, h).start()

    def far(h):
        z_copy(FAR, h).wait_recv()
        z_copy(FAR_SAME, h).start()

        @pl.when(helps)
        def _():
            x_query(h).wait_recv()
            m_s[1, h] = jnp.full((TOK, HD), NEGATIVE, F32)
            l_s[1, h] = jnp.zeros((TOK, HD), F32)
            acc_s[1, h] = jnp.zeros((TOK, HD), F32)

        @pl.when(ahead)
        def _():
            attend(0, h, 4, 1, 1)

        @pl.when(ahead & helps)
        def _():
            attend(1, h, 4, 1, 1)

    def far_same(h):
        z_copy(FAR_SAME, h).wait_recv()
        z_copy(FAR_LAST, h).start()
        attend(0, h, 5, 1, 0)

        @pl.when(helps)
        def _():
            attend(1, h, 5, 1, 0)

    def far_last(h):
        z_copy(FAR_LAST, h).wait_recv()

        @pl.when(helps & behind)
        def _():
            attend(1, h, 6, 1, 1)

        @pl.when(helps)
        def _():
            part_send[h] = (acc_s[1, h] / l_s[1, h]).astype(BF)
            x_part(h).start()
            lse = m_s[1, h] + jnp.log2(l_s[1, h])
            for block in range(TOK // HD):
                rows = slice(block * HD, (block + 1) * HD)
                lse_send[h, block : block + 1] = lse[rows].T[:1]
            x_lse(h).start()

        @pl.when(behind)
        def _():
            attend(0, h, 6, 1, 1)

        @pl.when(helps)
        def _():
            att[h] = (acc_s[0, h] / l_s[0, h]).astype(BF)
            spread(h)

    def merge(h):
        x_part(h).wait_recv()
        x_lse(h).wait_recv()
        for block in range(TOK // HD):
            rows = slice(block * HD, (block + 1) * HD)
            lse = jnp.broadcast_to(lse_recv[h, block : block + 1], (HD, HD)).T
            before = m_s[0, h, rows]
            peak = jnp.maximum(before, lse)
            fade, share = jnp.exp2(before - peak), jnp.exp2(lse - peak)
            total = fade * l_s[0, h, rows] + share
            mixed = fade * acc_s[0, h, rows] + share * part_recv[h, rows].astype(F32)
            att[h, rows] = (mixed / total).astype(BF)
        spread(h)

    def spread(h):
        for k in range(1, Y):
            y_copy(k, h).start()
        att_all[y, h] = att[h, pl.ds(pl.multiple_of(y * QUARTER, QUARTER), QUARTER)]

    each_head(hand_on)
    each_head(near)
    each_head(near_opposite)
    each_head(leap)
    each_head(far)
    each_head(far_same)
    for k in range(1, Y):
        w_copy(k).wait_recv()
        w_share(k).start()
    each_head(far_last)

    @pl.when(helped)
    def _():
        each_head(merge)

    for k in range(Y):
        w_share(k).wait_recv()
    last = HEADS_DEV - 1

    def project(h, cols):
        rows = pl.ds(pl.multiple_of(h * HD, HD), HD)
        total = jnp.dot(att_all[0, h], w_all[0, rows, cols], preferred_element_type=F32)
        for s in range(1, Y):
            total += jnp.dot(att_all[s, h], w_all[s, rows, cols], preferred_element_type=F32)
        return total

    for h in range(last):
        for k in range(1, Y):
            y_copy(k, h).wait_recv()
        for part in range(PARTS):
            cols = pl.ds(part * PART, PART)
            if h == 0:
                acc_o[:, cols] = project(h, cols)
            else:
                acc_o[:, cols] += project(h, cols)
    for k in range(1, Y):
        y_copy(k, last).wait_recv()
    for part in range(PARTS):
        cols = pl.ds(part * PART, PART)
        total = (acc_o[:, cols] + project(last, cols)).astype(BF)
        for piece in range(4):
            rows = slice(piece * OWN, (piece + 1) * OWN)
            send_o[part, piece, :OWN] = total[rows, : PART // 2]
            send_o[part, piece, OWN:] = total[rows, PART // 2 :]
        for k in (2, 3, 1):
            f_copy(k, part).start()

    own = xh * 2 + c
    for part in range(PARTS):
        for k in range(1, 4):
            f_copy(k, part).wait_recv()
        mine = send_o[part, own].astype(F32) + recv_o[part, 2].astype(F32)
        others = recv_o[part, 1].astype(F32) + recv_o[part, 3].astype(F32)
        mine, others = mine.astype(BF), others.astype(BF)
        for side in range(2):
            cols = pl.ds(part * PART + side * PART // 2, PART // 2)
            rows = slice(side * OWN, (side + 1) * OWN)
            out_ref[0, :, cols] = jnp.where(c == 0, mine[rows], others[rows])
            out_ref[1, :, cols] = jnp.where(c == 0, others[rows], mine[rows])

    def sent(h):
        for kind in range(len(ROUTES)):
            z_copy(kind, h).wait_send()

        @pl.when(helps)
        def _():
            x_part(h).wait_send()
            x_lse(h).wait_send()

        @pl.when(helped)
        def _():
            x_query(h).wait_send()

        for k in range(1, Y):
            y_copy(k, h).wait_send()

    each_head(sent)
    for k in range(1, Y):
        w_copy(k).wait_send()
    for k in range(Y):
        w_share(k).wait_send()
    for part in range(PARTS):
        for k in range(1, 4):
            f_copy(k, part).wait_send()


def local(query_rows, key_rows, value_rows, windows, out_weight):
    dma = pltpu.SemaphoreType.DMA
    anywhere = pl.BlockSpec(memory_space=pl.ANY)
    return pl.pallas_call(
        kernel,
        out_shape=jax.ShapeDtypeStruct((SEEDS, OWN, D), BF),
        in_specs=[anywhere] * 3 + [pl.BlockSpec(memory_space=pltpu.SMEM), anywhere],
        out_specs=pl.BlockSpec(memory_space=pltpu.VMEM),
        scratch_shapes=[
            pltpu.VMEM((SLOTS, HEADS_DEV, 2, TOK, HD), BF),
            pltpu.VMEM((2, HEADS_DEV, TOK, HD), BF),
            pltpu.VMEM((Y, 2 * W_ROWS, D), BF),
            pltpu.VMEM((HEADS_DEV, TOK, HD), BF),
            pltpu.VMEM((Y, HEADS_DEV, QUARTER, HD), BF),
            pltpu.VMEM((QUARTER, D), F32),
            pltpu.VMEM((PARTS, 4, 2 * OWN, PART // 2), BF),
            pltpu.VMEM((PARTS, 4, 2 * OWN, PART // 2), BF),
            pltpu.VMEM((2, HEADS_DEV, TOK, HD), F32),
            pltpu.VMEM((2, HEADS_DEV, TOK, HD), F32),
            pltpu.VMEM((2, HEADS_DEV, TOK, HD), F32),
            pltpu.VMEM((HEADS_DEV, TOK, HD), BF),
            pltpu.VMEM((HEADS_DEV, TOK, HD), BF),
            pltpu.VMEM((HEADS_DEV, 8, HD), F32),
            pltpu.VMEM((HEADS_DEV, 8, HD), F32),
            dma((4, HEADS_DEV)),
            dma((len(ROUTES), HEADS_DEV)),
            dma((len(ROUTES), HEADS_DEV)),
            dma((3, HEADS_DEV)),
            dma((3, HEADS_DEV)),
            dma((Y, HEADS_DEV)),
            dma((Y, HEADS_DEV)),
            dma((2 * Y,)),
            dma((2 * Y,)),
            dma((PARTS, 4)),
            dma((PARTS, 4)),
        ],
        compiler_params=pltpu.CompilerParams(
            collective_id=0, has_side_effects=True, vmem_limit_bytes=60 << 20
        ),
        cost_estimate=pl.CostEstimate(
            flops=2 * (2 * HEADS_DEV * TOK * 9 * TOK * HD + TOK * HEADS_DEV * HD * D),
            bytes_accessed=4 << 20,
            transcendentals=HEADS_DEV * TOK * 9 * TOK,
        ),
    )(query_rows, key_rows, value_rows, windows.T, out_weight)


def solution(mesh):
    placed = (P("frame", "head"), P("frame", "head"), P("frame", "head"), P(), P("head", None))
    return jax.shard_map(
        local,
        mesh=mesh,
        in_specs=placed,
        out_specs=P(None, ("frame", "head"), None),
        check_vma=False,
    )
```

time: 137 us -> 101 us (0.74); the launches traced: 134 us -> 101 us
  Pallas kernels: 128 us -> 98.9 us
  local copies, waits for them, and re-layouts: 5.63 us -> 1.69 us
    pallas_call x1, Pallas kernels: 128 us -> 98.9 us  [local(): pl.pallas_call(kernel, out_shape=jax.ShapeDtypeStruct((SEEDS, OWN, D), BF...]
    unnamed x10 -> x1, local copies, waits for them, and re-layouts: 5.63 us -> 1.69 us
where the time goes in v2:
time: 101 us
  Pallas kernels  98.9 us (98%)
  local copies, waits for them, and re-layouts  1.69 us (2%)
    pallas_call x1, Pallas kernels, local(): pl.pallas_call(kernel, out_shape=jax.ShapeDtypeStruct((SEEDS, OWN, D), BF...  98.9 us

profile of v2, /device:TPU:7, one launch (start us, length us, event | category | flops | bytes accessed | tf_op | source)
XLA Modules:
  0.0 100.6 jit_solution(5536860753445773825)
XLA Ops:
  0.0 98.9 %shard_map.55 = bf16[2,24,3072]{2,1,0:T(8,128)(2,1)} custom-call(bf16[384,384]{1,0:T(8,128)(2,1)} %q_hbm.1, bf16[384,384]{1,0:T(8,128)(2,1)} %k_hbm.1, bf16[384,384]{1,0:T(8,128)(2,1)} %v_hbm.1, s32[3,24]{1,0:T(4,128)} %bitcast.1, bf16[192,3072]{1,0:T(8,128)(2,1)} %w_hbm.1), custom_call_target="tpu_custom_call" | custom-call | flops 2944401408 | bytes 4194304 | tf_op jit(solution)/shard_map/pallas_call | solution.py:366
  98.9 1.7 %copy.7 = bf16[2,24,3072]{2,1,0:T(8,128)(2,1)} copy(bf16[2,24,3072]{2,1,0:T(8,128)(2,1)} %shard_map.55) | data formatting | bytes 589824

commit v3 on v2

v3 whole, which is shorter than its diff:
```python
import math

import jax
import jax.numpy as jnp
from jax import lax
from jax.experimental import pallas as pl
from jax.experimental.pallas import tpu as pltpu
from jax.sharding import PartitionSpec as P

HD = 128
SEEDS = 2
FRAME_TILES = 4
NEGATIVE = -1e30
VMEM = 56164352
MESH = pl.DeviceIdType.MESH
BF = jnp.bfloat16
F32 = jnp.float32

Z, Y = 16, 4
ROW_TILES = 8
HEADS_DEV = 3
TOK = 384
TILE = 192
D = 3072
W_ROWS = 192
OWN = 24
QUARTER = 96

CHAIN, OPPOSITE, LEAP, FAR, FAR_SAME, FAR_LAST = range(6)
ROUTES = ((0, 2, 1), (0, 1, -1), (2, 3, 3), (3, 4, 3), (4, 5, 1), (5, 6, 1))
SLOTS = 7
PIECES = 16
PIECE = 32
PARTS = 4
PART = D // PARTS
LOG2E = math.log2(math.e)
ATT, PARTIAL = range(2)


def kernel(q_hbm, k_hbm, v_hbm, windows, w_hbm, out_ref, *scratch):
    (kv, q_s, w_all, m_s, l_s, acc_s, att, part, att_in, part_in, acc_o, send_o, recv_o) = scratch[:13]
    (local_sem, z_send, z_recv, q_send, q_recv, a_send, a_recv, w_send, w_recv, f_send, f_recv) = scratch[13:]

    frame = lax.axis_index("frame")
    head = lax.axis_index("head")
    xl, z = frame // Z, frame % Z
    y, xh, c = head // 4, (head // 2) % 2, head % 2
    row = z % ROW_TILES
    upper = z // ROW_TILES
    step = 2 * c - 1
    helps = upper == xl
    helped = upper != xl

    def at_z(distance):
        return (xl * Z + (z + distance + Z) % Z, head)

    def at_owner(across, k):
        return ((xl + across) % 2 * Z + z, ((y + k) % Y) * 4 + xh * 2 + c)

    across_x = ((1 - xl) * Z + z, head)
    other_core = (frame, y * 4 + xh * 2 + 1 - c)

    def at_final(k):
        return (frame, y * 4 + (xh + k // 2) % 2 * 2 + (c + k) % 2)

    def local_copy(i, h):
        cols = pl.ds(pl.multiple_of(h * HD, HD), HD)
        source = (k_hbm, v_hbm, q_hbm)[i].at[:, cols]
        target = q_s.at[0, h] if i == 2 else kv.at[0, h, i]
        return pltpu.make_async_copy(source, target, local_sem.at[i, h])

    my_rows = pl.ds(pl.multiple_of(c * W_ROWS, W_ROWS), W_ROWS)
    w_local = pltpu.make_async_copy(w_hbm, w_all.at[y, my_rows], local_sem.at[3, 0])
    for i in range(3):
        for h in range(HEADS_DEV):
            local_copy(i, h).start()
    w_local.start()

    barrier = pltpu.get_barrier_semaphore()
    partners = [at_z(1), at_z(-1), at_z(3), at_z(-3), across_x]
    partners += [at_owner(0, 1), at_owner(0, 2), at_owner(0, 3), at_owner(1, 1), at_owner(1, 2), at_owner(1, 3), at_final(1), at_final(2), at_final(3)]
    for partner in partners:
        pl.semaphore_signal(barrier, inc=1, device_id=partner, device_id_type=MESH)
    pl.semaphore_wait(barrier, len(partners))

    def remote(src, dst, send, recv, target):
        return pltpu.make_async_remote_copy(
            src_ref=src, dst_ref=dst, send_sem=send, recv_sem=recv, device_id=target, device_id_type=MESH
        )

    def z_copy(kind, h):
        source, slot, hops = ROUTES[kind]
        return remote(
            kv.at[source, h], kv.at[slot, h], z_send.at[kind, h], z_recv.at[kind, h], at_z(hops * step)
        )

    def x_query(h):
        return remote(q_s.at[0, h], q_s.at[1, h], q_send.at[h], q_recv.at[h], across_x)

    def w_copy(k):
        return remote(w_hbm, w_all.at[y, my_rows], w_send.at[k], w_recv.at[k], at_owner(0, k))

    def w_share(k):
        place = w_all.at[(y + Y - k) % Y, my_rows]
        return remote(place, place, w_send.at[Y + k], w_recv.at[Y + k], other_core)

    def a_copy(kind, k, h):
        pieces = pl.ds((y + k) % Y * 4, 4)
        source, target = ((att, att_in), (part, part_in))[kind]
        sem = (kind, k, h)
        return remote(source.at[h, pieces], target.at[y, h], a_send.at[sem], a_recv.at[sem], at_owner(kind, k))

    def f_copy(k, part):
        piece = (xh + k // 2) % 2 * 2 + (c + k) % 2
        return remote(
            send_o.at[part, piece], recv_o.at[part, k], f_send.at[part, k], f_recv.at[part, k], at_final(k)
        )

    for h in range(HEADS_DEV):
        local_copy(0, h).wait()
        local_copy(1, h).wait()
        z_copy(CHAIN, h).start()
    for h in range(HEADS_DEV):
        z_copy(OPPOSITE, h).start()
    for h in range(HEADS_DEV):
        local_copy(2, h).wait()

        @pl.when(helped)
        def _():
            x_query(h).start()

    for k in range(1, Y):
        w_copy(k).start()
    w_local.wait()
    w_share(0).start()

    group = y * 2 + xh
    scaling = LOG2E / math.sqrt(HD)
    column = lax.broadcasted_iota(jnp.int32, (1, TOK), 1) // TILE

    ones = jnp.ones((TOK, HD), BF)

    def attend(owner, h, slot, far_frame, far_row, first=False):
        head_id = group * HEADS_DEV + h
        allowed = (far_frame <= windows[0, head_id]) & (far_row <= windows[1, head_id])
        same = jnp.where(allowed, 0.0, NEGATIVE)
        other = jnp.where(allowed & (windows[2, head_id] >= 1), 0.0, NEGATIVE)
        keys = kv[slot, h, 0]
        values = jnp.concatenate([kv[slot, h, 1], ones], axis=1)
        for half in range(2):
            rows = pl.ds(half * TILE, TILE)
            bias = jnp.where(column == half, same, other)
            scores = lax.dot_general(
                q_s[owner, h, rows], keys, (((1,), (1,)), ((), ())), preferred_element_type=F32
            )
            scores = scores * scaling + bias
            peak = jnp.max(scores, axis=1, keepdims=True)
            if not first:
                before = m_s[owner, h, rows, :1]
                peak = jnp.maximum(peak, before)
            weights = jnp.exp2(scores - peak)
            mixed = jnp.dot(weights.astype(BF), values, preferred_element_type=F32)
            mixed, total = mixed[:, :HD], mixed[:, HD:]
            if not first:
                fade = jnp.exp2(before - peak)
                total += fade * l_s[owner, h, rows]
                mixed += fade * acc_s[owner, h, rows]
            m_s[owner, h, rows] = jnp.broadcast_to(peak, (TILE, HD))
            l_s[owner, h, rows] = total
            acc_s[owner, h, rows] = mixed

    def in_grid(r):
        return (r >= 0) & (r < ROW_TILES)

    ahead, behind = in_grid(row + step), in_grid(row - step)

    def each_head(body):
        def run(h, carry):
            body(h)
            return carry

        lax.fori_loop(0, HEADS_DEV, run, 0)

    def hand_on(h):
        z_copy(CHAIN, h).wait_recv()
        z_copy(LEAP, h).start()

    def near(h):
        attend(0, h, 0, 0, 0, first=True)

        @pl.when(behind)
        def _():
            attend(0, h, 2, 0, 1)

    def near_opposite(h):
        z_copy(OPPOSITE, h).wait_recv()

        @pl.when(ahead)
        def _():
            attend(0, h, 1, 0, 1)

    def leap(h):
        z_copy(LEAP, h).wait_recv()
        z_copy(FAR, h).start()

    def far(h):
        z_copy(FAR, h).wait_recv()
        z_copy(FAR_SAME, h).start()

        @pl.when(helps)
        def _():
            x_query(h).wait_recv()
            m_s[1, h] = jnp.full((TOK, HD), NEGATIVE, F32)
            l_s[1, h] = jnp.zeros((TOK, HD), F32)
            acc_s[1, h] = jnp.zeros((TOK, HD), F32)

        @pl.when(ahead)
        def _():
            attend(0, h, 4, 1, 1)

        @pl.when(ahead & helps)
        def _():
            attend(1, h, 4, 1, 1)

    def far_same(h):
        z_copy(FAR_SAME, h).wait_recv()
        z_copy(FAR_LAST, h).start()
        attend(0, h, 5, 1, 0)

        @pl.when(helps)
        def _():
            attend(1, h, 5, 1, 0)

    def diagonal(size):
        shape = (size, HD)
        return lax.broadcasted_iota(jnp.int32, shape, 0) == lax.broadcasted_iota(jnp.int32, shape, 1)

    blank = jnp.zeros((PIECES, PIECE - OWN, HD), BF)
    mask = diagonal(OWN)

    def close(target, owner, h):
        mixed = acc_s[owner, h] / l_s[owner, h]
        target[h, :, :OWN] = mixed.reshape(PIECES, OWN, HD).astype(BF)

    def close_lse(target, owner, h):
        lse = m_s[owner, h] + jnp.log2(l_s[owner, h])
        lse = jnp.sum(jnp.where(mask, lse.reshape(PIECES, OWN, HD), 0.0), axis=1, keepdims=True)
        high = lse.astype(BF).astype(F32)
        middle = (lse - high).astype(BF).astype(F32)
        low = lse - high - middle
        place = lax.broadcasted_iota(jnp.int32, (PIECES, PIECE - OWN, HD), 1)
        lines = jnp.where(place == 0, high, jnp.where(place == 1, middle, jnp.where(place == 2, low, 0.0)))
        target[h, :, OWN:] = lines.astype(BF)

    def far_last(h):
        z_copy(FAR_LAST, h).wait_recv()

        @pl.when(helps)
        def _():
            @pl.when(behind)
            def _():
                attend(1, h, 6, 1, 1)

            close(part, 1, h)
            close_lse(part, 1, h)
            for k in (2, 1, 3, 0):
                a_copy(PARTIAL, k, h).start()
            att[h, :, OWN:] = blank

        @pl.when(behind)
        def _():
            attend(0, h, 6, 1, 1)

        close(att, 0, h)

        @pl.when(helped)
        def _():
            close_lse(att, 0, h)

        for k in (2, 1, 3):
            a_copy(ATT, k, h).start()
        att_in[y, h] = att[h, pl.ds(y * 4, 4)]

    def merged(own, other):
        own, other = own.astype(F32), other.astype(F32)

        def lse(piece):
            line = piece[:, OWN : OWN + 1] + piece[:, OWN + 1 : OWN + 2] + piece[:, OWN + 2 : OWN + 3]
            return jnp.sum(jnp.where(mask, line, 0.0), axis=2, keepdims=True)

        first, second = lse(own), lse(other)
        peak = jnp.maximum(first, second)
        first, second = jnp.exp2(first - peak), jnp.exp2(second - peak)
        total = first + second
        return ((first / total) * own[:, :OWN] + (second / total) * other[:, :OWN]).astype(BF)

    each_head(hand_on)
    each_head(near)
    each_head(near_opposite)
    each_head(leap)
    each_head(far)
    each_head(far_same)
    for k in range(1, Y):
        w_copy(k).wait_recv()
        w_share(k).start()
    each_head(far_last)

    for k in range(Y):
        w_share(k).wait_recv()
    last = HEADS_DEV - 1

    def arrived(h):
        for k in range(1, Y):
            a_copy(ATT, k, h).wait_recv()

        @pl.when(helped)
        def _():
            for k in range(Y):
                a_copy(PARTIAL, k, h).wait_recv()
            shape = (PIECES, PIECE, HD)
            joined = merged(att_in[:, h].reshape(shape), part_in[:, h].reshape(shape))
            att_in[:, h, :, :OWN] = joined.reshape(Y, 4, OWN, HD)

    def project(h, cols):
        rows = pl.ds(pl.multiple_of(h * HD, HD), HD)
        total = jnp.zeros((4 * PIECE, PART), F32)
        for s in range(Y):
            total += jnp.dot(
                att_in[s, h].reshape(4 * PIECE, HD), w_all[s, rows, cols], preferred_element_type=F32
            )
        return total

    for h in range(last):
        arrived(h)
        for part_index in range(PARTS):
            cols = pl.ds(part_index * PART, PART)
            if h == 0:
                acc_o[:, cols] = project(h, cols)
            else:
                acc_o[:, cols] += project(h, cols)
    arrived(last)
    for part_index in range(PARTS):
        cols = pl.ds(part_index * PART, PART)
        total = (acc_o[:, cols] + project(last, cols)).astype(BF)
        for piece in range(4):
            mine = total[piece * PIECE : piece * PIECE + OWN]
            send_o[part_index, piece, :OWN] = mine[:, : PART // 2]
            send_o[part_index, piece, OWN:] = mine[:, PART // 2 :]
        for k in (2, 3, 1):
            f_copy(k, part_index).start()

    own = xh * 2 + c
    for part_index in range(PARTS):
        for k in range(1, 4):
            f_copy(k, part_index).wait_recv()
        mine = send_o[part_index, own].astype(F32) + recv_o[part_index, 2].astype(F32)
        others = recv_o[part_index, 1].astype(F32) + recv_o[part_index, 3].astype(F32)
        mine, others = mine.astype(BF), others.astype(BF)
        for side in range(2):
            cols = pl.ds(part_index * PART + side * PART // 2, PART // 2)
            rows = slice(side * OWN, (side + 1) * OWN)
            out_ref[0, :, cols] = jnp.where(c == 0, mine[rows], others[rows])
            out_ref[1, :, cols] = jnp.where(c == 0, others[rows], mine[rows])

    def sent(h):
        for kind in range(len(ROUTES)):
            z_copy(kind, h).wait_send()

        @pl.when(helps)
        def _():
            for k in range(Y):
                a_copy(PARTIAL, k, h).wait_send()

        @pl.when(helped)
        def _():
            x_query(h).wait_send()

        for k in range(1, Y):
            a_copy(ATT, k, h).wait_send()

    each_head(sent)
    for k in range(1, Y):
        w_copy(k).wait_send()
    for k in range(Y):
        w_share(k).wait_send()
    for part_index in range(PARTS):
        for k in range(1, 4):
            f_copy(k, part_index).wait_send()


def local(query_rows, key_rows, value_rows, windows, out_weight):
    dma = pltpu.SemaphoreType.DMA
    anywhere = pl.BlockSpec(memory_space=pl.ANY)
    return pl.pallas_call(
        kernel,
        out_shape=jax.ShapeDtypeStruct((SEEDS, OWN, D), BF),
        in_specs=[anywhere] * 3 + [pl.BlockSpec(memory_space=pltpu.SMEM), anywhere],
        out_specs=pl.BlockSpec(memory_space=pltpu.VMEM),
        scratch_shapes=[
            pltpu.VMEM((SLOTS, HEADS_DEV, 2, TOK, HD), BF),
            pltpu.VMEM((2, HEADS_DEV, TOK, HD), BF),
            pltpu.VMEM((Y, 2 * W_ROWS, D), BF),
            pltpu.VMEM((2, HEADS_DEV, TOK, HD), F32),
            pltpu.VMEM((2, HEADS_DEV, TOK, HD), F32),
            pltpu.VMEM((2, HEADS_DEV, TOK, HD), F32),
            pltpu.VMEM((HEADS_DEV, PIECES, PIECE, HD), BF),
            pltpu.VMEM((HEADS_DEV, PIECES, PIECE, HD), BF),
            pltpu.VMEM((Y, HEADS_DEV, 4, PIECE, HD), BF),
            pltpu.VMEM((Y, HEADS_DEV, 4, PIECE, HD), BF),
            pltpu.VMEM((4 * PIECE, D), F32),
            pltpu.VMEM((PARTS, 4, 2 * OWN, PART // 2), BF),
            pltpu.VMEM((PARTS, 4, 2 * OWN, PART // 2), BF),
            dma((4, HEADS_DEV)),
            dma((len(ROUTES), HEADS_DEV)),
            dma((len(ROUTES), HEADS_DEV)),
            dma((HEADS_DEV,)),
            dma((HEADS_DEV,)),
            dma((2, Y, HEADS_DEV)),
            dma((2, Y, HEADS_DEV)),
            dma((2 * Y,)),
            dma((2 * Y,)),
            dma((PARTS, 4)),
            dma((PARTS, 4)),
        ],
        compiler_params=pltpu.CompilerParams(
            collective_id=0, has_side_effects=True, vmem_limit_bytes=VMEM
        ),
        cost_estimate=pl.CostEstimate(
            flops=2 * (2 * HEADS_DEV * TOK * 9 * TOK * HD + TOK * HEADS_DEV * HD * D),
            bytes_accessed=4 << 20,
            transcendentals=HEADS_DEV * TOK * 9 * TOK,
        ),
    )(query_rows, key_rows, value_rows, windows.T, out_weight)


def solution(mesh):
    placed = (P("frame", "head"), P("frame", "head"), P("frame", "head"), P(), P("head", None))
    return jax.shard_map(
        local,
        mesh=mesh,
        in_specs=placed,
        out_specs=P(None, ("frame", "head"), None),
        check_vma=False,
    )
```

time: 101 us -> 97.8 us (0.968)
  Pallas kernels: 98.9 us -> 95.2 us
    pallas_call x1, Pallas kernels: 98.9 us -> 95.2 us  [local(): pl.pallas_call(kernel, out_shape=jax.ShapeDtypeStruct((SEEDS, OWN, D), BF...]
where the time goes in v3:
time: 97.8 us; the launch traced here: 96.6 us
  Pallas kernels  95.2 us (97%)
  local copies, waits for them, and re-layouts  1.4 us (1%)
    pallas_call x1, Pallas kernels, local(): pl.pallas_call(kernel, out_shape=jax.ShapeDtypeStruct((SEEDS, OWN, D), BF...  95.2 us

profile of v3, /device:TPU:7, one launch (start us, length us, event | category | flops | bytes accessed | tf_op | source)
XLA Modules:
  0.0 96.6 jit_solution(9775954083879438605)
XLA Ops:
  0.0 0.0 copy-start
  0.0 0.7 copy-done
  0.7 95.2 %shard_map.55 = bf16[2,24,3072]{2,1,0:T(8,128)(2,1)S(1)} custom-call(bf16[384,384]{1,0:T(8,128)(2,1)} %q_hbm.1, bf16[384,384]{1,0:T(8,128)(2,1)} %k_hbm.1, bf16[384,384]{1,0:T(8,128)(2,1)} %v_hbm.1, s32[3,24]{1,0:T(4,128)S(1)} %bitcast.1, bf16[192,3072]{1,0:T(8,128)(2,1)} %w_hbm.1), custom_call_target="tpu_custom_call" | custom-call | flops 2944401408 | bytes 4194304 | tf_op jit(solution)/shard_map/pallas_call | solution.py:394
  95.9 0.7 copy.7
Async XLA Ops:
  0.0 0.7 copy-start

commit v4 on v3

--- a/solution.py
+++ b/solution.py
@@ -29,9 +29,8 @@
 CHAIN, OPPOSITE, LEAP, FAR, FAR_SAME, FAR_LAST = range(6)
 ROUTES = ((0, 2, 1), (0, 1, -1), (2, 3, 3), (3, 4, 3), (4, 5, 1), (5, 6, 1))
 SLOTS = 7
-PIECES = 16
-PIECE = 32
-PARTS = 4
+BLOCK = 112
+PARTS = 2
 PART = D // PARTS
 LOG2E = math.log2(math.e)
 ATT, PARTIAL = range(2)
@@ -51,17 +50,24 @@
     helps = upper == xl
     helped = upper != xl
 
-    def at_z(distance):
+    def z_place(distance):
         return (xl * Z + (z + distance + Z) % Z, head)
 
+    z_places = {hops: z_place(hops * step) for hops in (-3, -1, 1, 3)}
+
+    quarters = [(y + k) % Y for k in range(Y)]
+    owners = [[((xl + a) % 2 * Z + z, quarter * 4 + xh * 2 + c) for quarter in quarters] for a in range(2)]
+
     def at_owner(across, k):
-        return ((xl + across) % 2 * Z + z, ((y + k) % Y) * 4 + xh * 2 + c)
+        return owners[across][k]
 
     across_x = ((1 - xl) * Z + z, head)
     other_core = (frame, y * 4 + xh * 2 + 1 - c)
 
+    finals = [(frame, y * 4 + (xh + k // 2) % 2 * 2 + (c + k) % 2) for k in range(4)]
+
     def at_final(k):
-        return (frame, y * 4 + (xh + k // 2) % 2 * 2 + (c + k) % 2)
+        return finals[k]
 
     def local_copy(i, h):
         cols = pl.ds(pl.multiple_of(h * HD, HD), HD)
@@ -77,7 +83,7 @@
     w_local.start()
 
     barrier = pltpu.get_barrier_semaphore()
-    partners = [at_z(1), at_z(-1), at_z(3), at_z(-3), across_x]
+    partners = [z_places[1], z_places[-1], z_places[3], z_places[-3], across_x]
     partners += [at_owner(0, 1), at_owner(0, 2), at_owner(0, 3), at_owner(1, 1), at_owner(1, 2), at_owner(1, 3), at_final(1), at_final(2), at_final(3)]
     for partner in partners:
         pl.semaphore_signal(barrier, inc=1, device_id=partner, device_id_type=MESH)
@@ -91,7 +97,7 @@
     def z_copy(kind, h):
         source, slot, hops = ROUTES[kind]
         return remote(
-            kv.at[source, h], kv.at[slot, h], z_send.at[kind, h], z_recv.at[kind, h], at_z(hops * step)
+            kv.at[source, h], kv.at[slot, h], z_send.at[kind, h], z_recv.at[kind, h], z_places[hops]
         )
 
     def x_query(h):
@@ -101,14 +107,14 @@
         return remote(w_hbm, w_all.at[y, my_rows], w_send.at[k], w_recv.at[k], at_owner(0, k))
 
     def w_share(k):
-        place = w_all.at[(y + Y - k) % Y, my_rows]
+        place = w_all.at[quarters[-k % Y], my_rows]
         return remote(place, place, w_send.at[Y + k], w_recv.at[Y + k], other_core)
 
     def a_copy(kind, k, h):
-        pieces = pl.ds((y + k) % Y * 4, 4)
+        quarter = quarters[k]
         source, target = ((att, att_in), (part, part_in))[kind]
         sem = (kind, k, h)
-        return remote(source.at[h, pieces], target.at[y, h], a_send.at[sem], a_recv.at[sem], at_owner(kind, k))
+        return remote(source.at[h, quarter], target.at[y, h], a_send.at[sem], a_recv.at[sem], at_owner(kind, k))
 
     def f_copy(k, part):
         piece = (xh + k // 2) % 2 * 2 + (c + k) % 2
@@ -231,26 +237,25 @@
         def _():
             attend(1, h, 5, 1, 0)
 
-    def diagonal(size):
-        shape = (size, HD)
-        return lax.broadcasted_iota(jnp.int32, shape, 0) == lax.broadcasted_iota(jnp.int32, shape, 1)
-
-    blank = jnp.zeros((PIECES, PIECE - OWN, HD), BF)
-    mask = diagonal(OWN)
+    blank = jnp.zeros((BLOCK - QUARTER, HD), BF)
+    mask = lax.broadcasted_iota(jnp.int32, (QUARTER, HD), 0) == lax.broadcasted_iota(jnp.int32, (QUARTER, HD), 1)
 
     def close(target, owner, h):
-        mixed = acc_s[owner, h] / l_s[owner, h]
-        target[h, :, :OWN] = mixed.reshape(PIECES, OWN, HD).astype(BF)
+        mixed = (acc_s[owner, h] / l_s[owner, h]).astype(BF)
+        for quarter in range(Y):
+            target[h, quarter, :QUARTER] = mixed[quarter * QUARTER : (quarter + 1) * QUARTER]
 
     def close_lse(target, owner, h):
         lse = m_s[owner, h] + jnp.log2(l_s[owner, h])
-        lse = jnp.sum(jnp.where(mask, lse.reshape(PIECES, OWN, HD), 0.0), axis=1, keepdims=True)
-        high = lse.astype(BF).astype(F32)
-        middle = (lse - high).astype(BF).astype(F32)
-        low = lse - high - middle
-        place = lax.broadcasted_iota(jnp.int32, (PIECES, PIECE - OWN, HD), 1)
-        lines = jnp.where(place == 0, high, jnp.where(place == 1, middle, jnp.where(place == 2, low, 0.0)))
-        target[h, :, OWN:] = lines.astype(BF)
+        place = lax.broadcasted_iota(jnp.int32, (BLOCK - QUARTER, HD), 0)
+        for quarter in range(Y):
+            rows = lse[quarter * QUARTER : (quarter + 1) * QUARTER]
+            line = jnp.sum(jnp.where(mask, rows, 0.0), axis=0, keepdims=True)
+            high = line.astype(BF).astype(F32)
+            middle = (line - high).astype(BF).astype(F32)
+            low = line - high - middle
+            lines = jnp.where(place == 0, high, jnp.where(place == 1, middle, jnp.where(place == 2, low, 0.0)))
+            target[h, quarter, QUARTER:] = lines.astype(BF)
 
     def far_last(h):
         z_copy(FAR_LAST, h).wait_recv()
@@ -265,7 +270,8 @@
             close_lse(part, 1, h)
             for k in (2, 1, 3, 0):
                 a_copy(PARTIAL, k, h).start()
-            att[h, :, OWN:] = blank
+            for quarter in range(Y):
+                att[h, quarter, QUARTER:] = blank
 
         @pl.when(behind)
         def _():
@@ -279,20 +285,24 @@
 
         for k in (2, 1, 3):
             a_copy(ATT, k, h).start()
-        att_in[y, h] = att[h, pl.ds(y * 4, 4)]
+        att_in[y, h] = att[h, y]
 
     def merged(own, other):
-        own, other = own.astype(F32), other.astype(F32)
-
-        def lse(piece):
-            line = piece[:, OWN : OWN + 1] + piece[:, OWN + 1 : OWN + 2] + piece[:, OWN + 2 : OWN + 3]
-            return jnp.sum(jnp.where(mask, line, 0.0), axis=2, keepdims=True)
+        def lse(block):
+            lines = block[QUARTER:].astype(F32)
+            return lines[0:1] + lines[1:2] + lines[2:3]
 
         first, second = lse(own), lse(other)
         peak = jnp.maximum(first, second)
         first, second = jnp.exp2(first - peak), jnp.exp2(second - peak)
         total = first + second
-        return ((first / total) * own[:, :OWN] + (second / total) * other[:, :OWN]).astype(BF)
+        shares = []
+        for share in (first / total, second / total):
+            high = share.astype(BF).astype(F32)
+            shares += [jnp.where(mask, line, 0.0).astype(BF) for line in (high, share - high)]
+        pad = jnp.zeros((HD - BLOCK, HD), BF)
+        both_results = jnp.concatenate([own, pad, own, pad, other, pad, other, pad], axis=0)
+        return jnp.dot(jnp.concatenate(shares, axis=1), both_results, preferred_element_type=F32).astype(BF)
 
     each_head(hand_on)
     each_head(near)
@@ -317,16 +327,15 @@
         def _():
             for k in range(Y):
                 a_copy(PARTIAL, k, h).wait_recv()
-            shape = (PIECES, PIECE, HD)
-            joined = merged(att_in[:, h].reshape(shape), part_in[:, h].reshape(shape))
-            att_in[:, h, :, :OWN] = joined.reshape(Y, 4, OWN, HD)
+            for s in range(Y):
+                att_in[s, h, :QUARTER] = merged(att_in[s, h], part_in[s, h])
 
     def project(h, cols):
         rows = pl.ds(pl.multiple_of(h * HD, HD), HD)
-        total = jnp.zeros((4 * PIECE, PART), F32)
+        total = jnp.zeros((QUARTER, PART), F32)
         for s in range(Y):
             total += jnp.dot(
-                att_in[s, h].reshape(4 * PIECE, HD), w_all[s, rows, cols], preferred_element_type=F32
+                att_in[s, h, :QUARTER], w_all[s, rows, cols], preferred_element_type=F32
             )
         return total
 
@@ -343,11 +352,33 @@
         cols = pl.ds(part_index * PART, PART)
         total = (acc_o[:, cols] + project(last, cols)).astype(BF)
         for piece in range(4):
-            mine = total[piece * PIECE : piece * PIECE + OWN]
+            mine = total[piece * OWN : (piece + 1) * OWN]
             send_o[part_index, piece, :OWN] = mine[:, : PART // 2]
             send_o[part_index, piece, OWN:] = mine[:, PART // 2 :]
         for k in (2, 3, 1):
             f_copy(k, part_index).start()
+
+    def sent(h):
+        for kind in range(len(ROUTES)):
+            z_copy(kind, h).wait_send()
+
+        @pl.when(helps)
+        def _():
+            for k in range(Y):
+                a_copy(PARTIAL, k, h).wait_send()
+
+        @pl.when(helped)
+        def _():
+            x_query(h).wait_send()
+
+        for k in range(1, Y):
+            a_copy(ATT, k, h).wait_send()
+
+    each_head(sent)
+    for k in range(1, Y):
+        w_copy(k).wait_send()
+    for k in range(Y):
+        w_share(k).wait_send()
 
     own = xh * 2 + c
     for part_index in range(PARTS):
@@ -362,27 +393,6 @@
             out_ref[0, :, cols] = jnp.where(c == 0, mine[rows], others[rows])
             out_ref[1, :, cols] = jnp.where(c == 0, others[rows], mine[rows])
 
-    def sent(h):
-        for kind in range(len(ROUTES)):
-            z_copy(kind, h).wait_send()
-
-        @pl.when(helps)
-        def _():
-            for k in range(Y):
-                a_copy(PARTIAL, k, h).wait_send()
-
-        @pl.when(helped)
-        def _():
-            x_query(h).wait_send()
-
-        for k in range(1, Y):
-            a_copy(ATT, k, h).wait_send()
-
-    each_head(sent)
-    for k in range(1, Y):
-        w_copy(k).wait_send()
-    for k in range(Y):
-        w_share(k).wait_send()
     for part_index in range(PARTS):
         for k in range(1, 4):
             f_copy(k, part_index).wait_send()
@@ -403,11 +413,11 @@
             pltpu.VMEM((2, HEADS_DEV, TOK, HD), F32),
             pltpu.VMEM((2, HEADS_DEV, TOK, HD), F32),
             pltpu.VMEM((2, HEADS_DEV, TOK, HD), F32),
-            pltpu.VMEM((HEADS_DEV, PIECES, PIECE, HD), BF),
-            pltpu.VMEM((HEADS_DEV, PIECES, PIECE, HD), BF),
-            pltpu.VMEM((Y, HEADS_DEV, 4, PIECE, HD), BF),
-            pltpu.VMEM((Y, HEADS_DEV, 4, PIECE, HD), BF),
-            pltpu.VMEM((4 * PIECE, D), F32),
+            pltpu.VMEM((HEADS_DEV, Y, BLOCK, HD), BF),
+            pltpu.VMEM((HEADS_DEV, Y, BLOCK, HD), BF),
+            pltpu.VMEM((Y, HEADS_DEV, BLOCK, HD), BF),
+            pltpu.VMEM((Y, HEADS_DEV, BLOCK, HD), BF),
+            pltpu.VMEM((QUARTER, D), F32),
             pltpu.VMEM((PARTS, 4, 2 * OWN, PART // 2), BF),
             pltpu.VMEM((PARTS, 4, 2 * OWN, PART // 2), BF),
             dma((4, HEADS_DEV)),

time: 97.8 us -> 96.9 us (level)
  no operation moved by 1% of the time
where the time goes in v4:
time: 96.9 us; the launch traced here: 95.9 us
  Pallas kernels  94.5 us (98%)
  local copies, waits for them, and re-layouts  1.4 us (1%)
    pallas_call x1, Pallas kernels, local(): pl.pallas_call(kernel, out_shape=jax.ShapeDtypeStruct((SEEDS, OWN, D), BF...  94.5 us

profile of v4, /device:TPU:7, one launch (start us, length us, event | category | flops | bytes accessed | tf_op | source)
XLA Modules:
  0.0 95.9 jit_solution(3083752023076279513)
XLA Ops:
  0.0 0.0 copy-start
  0.0 0.7 copy-done
  0.7 94.5 %shard_map.55 = bf16[2,24,3072]{2,1,0:T(8,128)(2,1)S(1)} custom-call(bf16[384,384]{1,0:T(8,128)(2,1)} %q_hbm.1, bf16[384,384]{1,0:T(8,128)(2,1)} %k_hbm.1, bf16[384,384]{1,0:T(8,128)(2,1)} %v_hbm.1, s32[3,24]{1,0:T(4,128)S(1)} %bitcast.1, bf16[192,3072]{1,0:T(8,128)(2,1)} %w_hbm.1), custom_call_target="tpu_custom_call" | custom-call | flops 2944401408 | bytes 4194304 | tf_op jit(solution)/shard_map/pallas_call | solution.py:404
  95.1 0.7 copy.7
Async XLA Ops:
  0.0 0.7 copy-start

commit v5 on v4

--- a/solution.py
+++ b/solution.py
@@ -26,9 +26,9 @@
 OWN = 24
 QUARTER = 96
 
-CHAIN, OPPOSITE, LEAP, FAR, FAR_SAME, FAR_LAST = range(6)
-ROUTES = ((0, 2, 1), (0, 1, -1), (2, 3, 3), (3, 4, 3), (4, 5, 1), (5, 6, 1))
-SLOTS = 7
+CHAIN, OPPOSITE, LEAP, LEAP_ON, FAR, FAR_SAME, FAR_LAST = range(7)
+ROUTES = ((0, 2, 1), (0, 1, -1), (2, 3, 2), (3, 4, 2), (4, 5, 2), (5, 6, 1), (6, 7, 1))
+SLOTS = 8
 BLOCK = 112
 PARTS = 2
 PART = D // PARTS
@@ -36,9 +36,10 @@
 ATT, PARTIAL = range(2)
 
 
-def kernel(q_hbm, k_hbm, v_hbm, windows, w_hbm, out_ref, *scratch):
+def kernel(q_hbm, k_hbm, v_hbm, windows_hbm, w_hbm, out_ref, *scratch):
     (kv, q_s, w_all, m_s, l_s, acc_s, att, part, att_in, part_in, acc_o, send_o, recv_o) = scratch[:13]
-    (local_sem, z_send, z_recv, q_send, q_recv, a_send, a_recv, w_send, w_recv, f_send, f_recv) = scratch[13:]
+    (local_sem, z_send, z_recv, q_send, q_recv, a_send, a_recv, w_send, w_recv, f_send, f_recv) = scratch[13:-1]
+    windows = scratch[-1]
 
     frame = lax.axis_index("frame")
     head = lax.axis_index("head")
@@ -53,7 +54,7 @@
     def z_place(distance):
         return (xl * Z + (z + distance + Z) % Z, head)
 
-    z_places = {hops: z_place(hops * step) for hops in (-3, -1, 1, 3)}
+    z_places = {hops: z_place(hops * step) for hops in (-2, -1, 1, 2)}
 
     quarters = [(y + k) % Y for k in range(Y)]
     owners = [[((xl + a) % 2 * Z + z, quarter * 4 + xh * 2 + c) for quarter in quarters] for a in range(2)]
@@ -77,13 +78,15 @@
 
     my_rows = pl.ds(pl.multiple_of(c * W_ROWS, W_ROWS), W_ROWS)
     w_local = pltpu.make_async_copy(w_hbm, w_all.at[y, my_rows], local_sem.at[3, 0])
+    windows_copy = pltpu.make_async_copy(windows_hbm, windows, local_sem.at[3, 1])
+    windows_copy.start()
     for i in range(3):
         for h in range(HEADS_DEV):
             local_copy(i, h).start()
     w_local.start()
 
     barrier = pltpu.get_barrier_semaphore()
-    partners = [z_places[1], z_places[-1], z_places[3], z_places[-3], across_x]
+    partners = [z_places[1], z_places[-1], z_places[2], z_places[-2], across_x]
     partners += [at_owner(0, 1), at_owner(0, 2), at_owner(0, 3), at_owner(1, 1), at_owner(1, 2), at_owner(1, 3), at_final(1), at_final(2), at_final(3)]
     for partner in partners:
         pl.semaphore_signal(barrier, inc=1, device_id=partner, device_id_type=MESH)
@@ -140,6 +143,7 @@
     w_local.wait()
     w_share(0).start()
 
+    windows_copy.wait()
     group = y * 2 + xh
     scaling = LOG2E / math.sqrt(HD)
     column = lax.broadcasted_iota(jnp.int32, (1, TOK), 1) // TILE
@@ -207,6 +211,10 @@
 
     def leap(h):
         z_copy(LEAP, h).wait_recv()
+        z_copy(LEAP_ON, h).start()
+
+    def leap_on(h):
+        z_copy(LEAP_ON, h).wait_recv()
         z_copy(FAR, h).start()
 
     def far(h):
@@ -222,20 +230,20 @@
 
         @pl.when(ahead)
         def _():
-            attend(0, h, 4, 1, 1)
+            attend(0, h, 5, 1, 1)
 
         @pl.when(ahead & helps)
         def _():
-            attend(1, h, 4, 1, 1)
+            attend(1, h, 5, 1, 1)
 
     def far_same(h):
         z_copy(FAR_SAME, h).wait_recv()
         z_copy(FAR_LAST, h).start()
-        attend(0, h, 5, 1, 0)
+        attend(0, h, 6, 1, 0)
 
         @pl.when(helps)
         def _():
-            attend(1, h, 5, 1, 0)
+            attend(1, h, 6, 1, 0)
 
     blank = jnp.zeros((BLOCK - QUARTER, HD), BF)
     mask = lax.broadcasted_iota(jnp.int32, (QUARTER, HD), 0) == lax.broadcasted_iota(jnp.int32, (QUARTER, HD), 1)
@@ -264,7 +272,7 @@
         def _():
             @pl.when(behind)
             def _():
-                attend(1, h, 6, 1, 1)
+                attend(1, h, 7, 1, 1)
 
             close(part, 1, h)
             close_lse(part, 1, h)
@@ -275,7 +283,7 @@
 
         @pl.when(behind)
         def _():
-            attend(0, h, 6, 1, 1)
+            attend(0, h, 7, 1, 1)
 
         close(att, 0, h)
 
@@ -308,6 +316,7 @@
     each_head(near)
     each_head(near_opposite)
     each_head(leap)
+    each_head(leap_on)
     each_head(far)
     each_head(far_same)
     for k in range(1, Y):
@@ -404,7 +413,7 @@
     return pl.pallas_call(
         kernel,
         out_shape=jax.ShapeDtypeStruct((SEEDS, OWN, D), BF),
-        in_specs=[anywhere] * 3 + [pl.BlockSpec(memory_space=pltpu.SMEM), anywhere],
+        in_specs=[anywhere] * 5,
         out_specs=pl.BlockSpec(memory_space=pltpu.VMEM),
         scratch_shapes=[
             pltpu.VMEM((SLOTS, HEADS_DEV, 2, TOK, HD), BF),
@@ -431,6 +440,7 @@
             dma((2 * Y,)),
             dma((PARTS, 4)),
             dma((PARTS, 4)),
+            pltpu.SMEM((3, 24), jnp.int32),
         ],
         compiler_params=pltpu.CompilerParams(
             collective_id=0, has_side_effects=True, vmem_limit_bytes=VMEM

time: 96.9 us -> 95.9 us (0.990)
  no operation moved by 1% of the time
where the time goes in v5:
time: 95.9 us; the launch traced here: 95.7 us
  Pallas kernels  94.3 us (98%)
  local copies, waits for them, and re-layouts  1.4 us (1%)
    pallas_call x1, Pallas kernels, local(): pl.pallas_call(kernel, out_shape=jax.ShapeDtypeStruct((SEEDS, OWN, D), BF...  94.3 us

profile of v5, /device:TPU:7, one launch (start us, length us, event | category | flops | bytes accessed | tf_op | source)
XLA Modules:
  0.0 95.7 jit_solution(6007625091850747474)
XLA Ops:
  0.0 0.0 copy-start
  0.0 0.7 copy-done
  0.7 94.3 %shard_map.55 = bf16[2,24,3072]{2,1,0:T(8,128)(2,1)S(1)} custom-call(bf16[384,384]{1,0:T(8,128)(2,1)} %q_hbm.1, bf16[384,384]{1,0:T(8,128)(2,1)} %k_hbm.1, bf16[384,384]{1,0:T(8,128)(2,1)} %v_hbm.1, s32[3,24]{1,0:T(4,128)S(1)} %bitcast.1, bf16[192,3072]{1,0:T(8,128)(2,1)} %w_hbm.1), custom_call_target="tpu_custom_call" | custom-call | flops 2944401408 | bytes 4194304 | tf_op jit(solution)/shard_map/pallas_call | solution.py:413
  95.0 0.7 copy.7
Async XLA Ops:
  0.0 0.7 copy-start

commit v6 on v5

--- a/solution.py
+++ b/solution.py
@@ -78,6 +78,13 @@
 
     my_rows = pl.ds(pl.multiple_of(c * W_ROWS, W_ROWS), W_ROWS)
     w_local = pltpu.make_async_copy(w_hbm, w_all.at[y, my_rows], local_sem.at[3, 0])
+
+    barrier = pltpu.get_barrier_semaphore()
+    partners = [z_places[1], z_places[-1], z_places[2], z_places[-2], across_x]
+    partners += [at_owner(0, 1), at_owner(0, 2), at_owner(0, 3), at_owner(1, 1), at_owner(1, 2), at_owner(1, 3), at_final(1), at_final(2), at_final(3)]
+    for partner in partners:
+        pl.semaphore_signal(barrier, inc=1, device_id=partner, device_id_type=MESH)
+
     windows_copy = pltpu.make_async_copy(windows_hbm, windows, local_sem.at[3, 1])
     windows_copy.start()
     for i in range(3):
@@ -85,11 +92,6 @@
             local_copy(i, h).start()
     w_local.start()
 
-    barrier = pltpu.get_barrier_semaphore()
-    partners = [z_places[1], z_places[-1], z_places[2], z_places[-2], across_x]
-    partners += [at_owner(0, 1), at_owner(0, 2), at_owner(0, 3), at_owner(1, 1), at_owner(1, 2), at_owner(1, 3), at_final(1), at_final(2), at_final(3)]
-    for partner in partners:
-        pl.semaphore_signal(barrier, inc=1, device_id=partner, device_id_type=MESH)
     pl.semaphore_wait(barrier, len(partners))
 
     def remote(src, dst, send, recv, target):

time: 95.9 us -> 95.9 us (level)
  no operation moved by 1% of the time
where the time goes in v6:
time: 95.9 us; the launch traced here: 95.7 us
  Pallas kernels  94.3 us (98%)
  local copies, waits for them, and re-layouts  1.4 us (1%)
    pallas_call x1, Pallas kernels, local(): pl.pallas_call(kernel, out_shape=jax.ShapeDtypeStruct((SEEDS, OWN, D), BF...  94.3 us

profile of v6, /device:TPU:7, one launch (start us, length us, event | category | flops | bytes accessed | tf_op | source)
XLA Modules:
  0.0 95.7 jit_solution(14203335497581167950)
XLA Ops:
  0.0 0.0 copy-start
  0.0 0.7 copy-done
  0.7 94.3 %shard_map.55 = bf16[2,24,3072]{2,1,0:T(8,128)(2,1)S(1)} custom-call(bf16[384,384]{1,0:T(8,128)(2,1)} %q_hbm.1, bf16[384,384]{1,0:T(8,128)(2,1)} %k_hbm.1, bf16[384,384]{1,0:T(8,128)(2,1)} %v_hbm.1, s32[3,24]{1,0:T(4,128)S(1)} %bitcast.1, bf16[192,3072]{1,0:T(8,128)(2,1)} %w_hbm.1), custom_call_target="tpu_custom_call" | custom-call | flops 2944401408 | bytes 4194304 | tf_op jit(solution)/shard_map/pallas_call | solution.py:415
  95.0 0.7 copy.7
Async XLA Ops:
  0.0 0.7 copy-start
